TPU v7x, 128 devices: a whole 4x4x4 slice. The times are simulated.
128 devices in a mesh: section: 2 (over core), expert: 16 (over y, x), shard: 4 (over z).
Axes of the slice: x: 4, y: 4, z: 4, core: 2. Of those that a mesh axis runs over, the one named last changes fastest.
Arguments:
- inputs: float32 [2, 16, 256, 768], P(None, 'expert', 'shard'), may hold values from -6 to 6
- cotangent: float32 [2, 16, 256, 768], P(None, 'expert', 'shard'), may hold values from -6 to 6
- w_qkv: bfloat16 [2, 768, 2304], P('section', 'shard'), may hold values from -0.21875 to 0.21875
- w_attn: bfloat16 [2, 768, 768], P('section', 'shard'), may hold values from -0.875 to 0.875
- gain_one: bfloat16 [2, 768], P('section', 'shard'), may hold values from 0.5 to 1.5
- gain_two: bfloat16 [2, 768], P('section', 'shard'), may hold values from 0.5 to 1.5
- router: bfloat16 [2, 768, 32], P('section', 'shard'), may hold values from -0.15625 to 0.15625
- w_in: bfloat16 [2, 32, 768, 3072], P('section', 'expert', None, 'shard'), may hold values from -0.21875 to 0.21875
- w_out: bfloat16 [2, 32, 3072, 768], P('section', 'expert', 'shard'), may hold values from -0.109375 to 0.109375
- routes: int32 [2, 2, 16, 4, 64, 2], P('section', None, 'expert', 'shard'), may hold values from 0 to 31, all different within a row; in each aligned block of 64 rows (0 to 63, 64 to 127, ..., all dimensions but the last counted through in order) at most 5 rows name the same one
Outputs:
- activations: float32 [2, 2, 16, 256, 768], P('section', None, 'expert', 'shard')
- input_grads: float32 [2, 2, 16, 256, 768], P('section', None, 'expert', 'shard')
- grad_qkv: float32 [2, 768, 2304], P('section', ('expert', 'shard'))
- grad_attn: float32 [2, 768, 768], P('section', ('expert', 'shard'))
- grad_gain_one: float32 [2, 768], P('section', ('expert', 'shard'))
- grad_gain_two: float32 [2, 768], P('section', ('expert', 'shard'))
- grad_router: float32 [2, 768, 32], P('section', ('expert', 'shard'))
- grad_in: float32 [2, 32, 768, 3072], P('section', 'expert', None, 'shard')
- grad_out: float32 [2, 32, 3072, 768], P('section', 'expert', 'shard')
Inputs may be any that keep to these rules, and one draw needn't show every extreme that they name: `routes`: each token names two different experts. In each aligned block of 64 tokens (one section, micro-batch, image group and position group) no expert is named more than 5 times, a bound that some block reaches.
All inputs are finite; a program needn't handle non-finite values.
Results may differ from a plain program's by a relative error of at most 0.03.
Values may be sent and summed in bfloat16 or wider, within the bound.
No kernel may reach another device: no remote copies, remote signals or barrier semaphores. Data moves between devices by JAX's collectives and lax.ppermute only.
A program may use at most 192 MiB of HBM per device.

v0:
```python
import math

import jax
import jax.numpy as jnp
from jax import lax
from jax.sharding import PartitionSpec as P

HEADS = 12
HDIM = 64


precise = lax.Precision.HIGHEST


def from_behind(value, axis, by):
    count = lax.axis_size(axis)
    pairs = [(i, i + by) for i in range(count) if 0 <= i + by < count]
    return lax.ppermute(value, axis, pairs)


def layer_norm(token_rows, gain_vec):
    row_mean = jnp.mean(token_rows, -1, keepdims=True)
    centered = token_rows - row_mean
    spread = jnp.mean(centered * centered, -1, keepdims=True)
    return centered * lax.rsqrt(spread + 1e-06) * gain_vec


def split_pair(values):
    upper = values.astype(jnp.bfloat16)
    lower = (values - upper.astype(jnp.float32)).astype(jnp.bfloat16)
    return (upper, lower)


def wide_left(form, wide, narrow):
    upper, lower = split_pair(wide)
    first = jnp.einsum(form, upper, narrow, preferred_element_type=jnp.float32)
    return first + jnp.einsum(form, lower, narrow, preferred_element_type=jnp.float32)


def wide_right(form, narrow, wide):
    upper, lower = split_pair(wide)
    first = jnp.einsum(form, narrow, upper, preferred_element_type=jnp.float32)
    return first + jnp.einsum(form, narrow, lower, preferred_element_type=jnp.float32)


def slot_table(route_ids, experts, capacity):
    flat_ids = route_ids.reshape(-1)
    onehot = (flat_ids[:, None] == jnp.arange(experts, dtype=jnp.int32)[None, :]).astype(jnp.int32)
    before = jnp.cumsum(onehot, 0) - onehot
    slot_ids = jnp.sum(before * onehot, 1)
    slot_index = flat_ids * capacity + slot_ids
    placement = (
        slot_index[:, None] == jnp.arange(experts * capacity, dtype=jnp.int32)[None, :]
    ).astype(jnp.float32)
    return placement.reshape(route_ids.shape[0], 2, experts * capacity)


def attention_scores(query, all_keys):
    score_scale = 1.0 / math.sqrt(HDIM)
    return (
        jnp.einsum("isha,itha->ihst", query, all_keys, preferred_element_type=jnp.float32)
        * score_scale
    )


def forward_block(block_in, gathered, expert_in, expert_out, route_ids):
    qkv_w, attn_w, gain_a, gain_b, router_w = gathered
    images, local_seq, model_width = block_in.shape
    token_count = images * local_seq
    experts = router_w.shape[1]
    capacity = max(2, (10 * token_count + 4 * experts - 1) // (4 * experts))
    token_rows = block_in.reshape(token_count, model_width)
    normed_a = layer_norm(token_rows, gain_a.astype(jnp.float32)).astype(jnp.bfloat16)
    projected = jnp.dot(normed_a, qkv_w, preferred_element_type=jnp.float32).astype(jnp.bfloat16)
    query = projected[:, :model_width].reshape(images, local_seq, HEADS, HDIM)
    key_local = projected[:, model_width : 2 * model_width].reshape(images, local_seq, HEADS, HDIM)
    value_local = projected[:, 2 * model_width :].reshape(images, local_seq, HEADS, HDIM)
    all_keys, all_values = (
        lax.all_gather(key_local, "shard", axis=1, tiled=True),
        lax.all_gather(value_local, "shard", axis=1, tiled=True),
    )
    scores = attention_scores(query, all_keys)
    row_top = jnp.max(scores, -1, keepdims=True)
    log_total = row_top + jnp.log(jnp.sum(jnp.exp(scores - row_top), -1, keepdims=True))
    attn_probs = jnp.exp(scores - log_total).astype(jnp.bfloat16)
    attended = jnp.einsum(
        "ihst,itha->isha", attn_probs, all_values, preferred_element_type=jnp.float32
    )
    attended = attended.reshape(token_count, model_width).astype(jnp.bfloat16)
    middle = token_rows + jnp.dot(attended, attn_w, preferred_element_type=jnp.float32)
    normed_b = layer_norm(middle, gain_b.astype(jnp.float32)).astype(jnp.bfloat16)
    logits = jnp.dot(normed_b, router_w, preferred_element_type=jnp.float32)
    placement = slot_table(route_ids, experts, capacity)
    select = jnp.sum(placement.reshape(token_count, 2, experts, capacity), -1)
    chosen = jnp.sum(select * logits[:, None, :], -1)
    gate_values = jax.nn.softmax(chosen, -1)
    taken_slots = jnp.sum(placement, 1).astype(jnp.bfloat16)
    outgoing = jnp.einsum("tc,td->cd", taken_slots, normed_b, preferred_element_type=jnp.float32)
    outgoing = outgoing.astype(jnp.bfloat16).reshape(experts, capacity, model_width)
    arrived = lax.all_to_all(outgoing, "expert", split_axis=0, concat_axis=1, tiled=True)
    expert_rows = lax.all_gather(arrived, "shard", axis=1, tiled=True)
    expert_up = jnp.einsum(
        "end,edf->enf", expert_rows, expert_in, preferred_element_type=jnp.float32
    )
    hidden = jax.nn.gelu(expert_up, approximate=False).astype(jnp.bfloat16)
    partial_out = jnp.einsum("enf,efd->end", hidden, expert_out, preferred_element_type=jnp.float32)
    summed = lax.psum_scatter(
        partial_out.astype(jnp.bfloat16), "shard", scatter_dimension=1, tiled=True
    )
    returned = lax.all_to_all(summed, "expert", split_axis=1, concat_axis=0, tiled=True)
    returned = returned.reshape(experts * capacity, model_width)
    mixing = jnp.sum(placement * gate_values[:, :, None], 1)
    combined = wide_left("tc,cd->td", mixing, returned)
    result = (middle + combined).reshape(block_in.shape)
    kept_state = (
        token_rows,
        normed_a,
        query,
        all_keys,
        all_values,
        log_total,
        attended,
        middle,
        normed_b,
        chosen,
        placement,
        expert_rows,
        expert_up,
        hidden,
        returned,
    )
    return (result, kept_state)


def backward_block(grad_output, kept_state, gathered, expert_in, expert_out):
    (
        token_rows,
        normed_a,
        query,
        all_keys,
        all_values,
        log_total,
        attended,
        middle,
        normed_b,
        chosen,
        placement,
        expert_rows,
        expert_up,
        hidden,
        returned,
    ) = kept_state
    qkv_w, attn_w, gain_a, gain_b, router_w = gathered
    images, local_seq = (query.shape[0], query.shape[1])
    token_count, model_width = token_rows.shape
    experts = router_w.shape[1]
    capacity = placement.shape[2] // experts
    grad_rows = grad_output.reshape(token_count, model_width)
    gate_values, gate_back = jax.vjp(lambda logit_pair: jax.nn.softmax(logit_pair, -1), chosen)
    mixing = jnp.sum(placement * gate_values[:, :, None], 1)
    grad_returned = jnp.einsum("tc,td->cd", mixing, grad_rows, precision=precise)
    grad_returned = grad_returned.astype(jnp.bfloat16).reshape(experts, capacity, model_width)
    grad_mixing = wide_left("td,cd->tc", grad_rows, returned)
    grad_gates = jnp.sum(placement * grad_mixing[:, None, :], -1)
    (grad_chosen,) = gate_back(grad_gates)
    select = jnp.sum(placement.reshape(token_count, 2, experts, capacity), -1)
    grad_logits = jnp.sum(select * grad_chosen[:, :, None], 1)
    grad_router = wide_right("td,te->de", normed_b, grad_logits)
    grad_normed = wide_left("te,de->td", grad_logits, router_w)
    arriving = lax.all_to_all(grad_returned, "expert", split_axis=0, concat_axis=1, tiled=True)
    slot_grads = lax.all_gather(arriving, "shard", axis=1, tiled=True)
    grad_expert_out = jnp.einsum(
        "enf,end->efd", hidden, slot_grads, preferred_element_type=jnp.float32
    )
    grad_hidden = jnp.einsum(
        "end,efd->enf", slot_grads, expert_out, preferred_element_type=jnp.float32
    )
    _, gelu_back = jax.vjp(lambda pre_act: jax.nn.gelu(pre_act, approximate=False), expert_up)
    (grad_up,) = gelu_back(grad_hidden)
    grad_up = grad_up.astype(jnp.bfloat16)
    grad_expert_in = jnp.einsum(
        "end,enf->edf", expert_rows, grad_up, preferred_element_type=jnp.float32
    )
    grad_part = jnp.einsum("enf,edf->end", grad_up, expert_in, preferred_element_type=jnp.float32)
    grad_slots = lax.psum_scatter(
        grad_part.astype(jnp.bfloat16), "shard", scatter_dimension=1, tiled=True
    )
    grad_sent = lax.all_to_all(grad_slots, "expert", split_axis=1, concat_axis=0, tiled=True)
    grad_sent = grad_sent.reshape(experts * capacity, model_width)
    taken_slots = jnp.sum(placement, 1).astype(jnp.bfloat16)
    grad_normed = grad_normed + jnp.dot(taken_slots, grad_sent, preferred_element_type=jnp.float32)
    _, second_back = jax.vjp(layer_norm, middle, gain_b.astype(jnp.float32))
    grad_middle_norm, grad_gain_b = second_back(grad_normed)
    grad_middle = grad_rows + grad_middle_norm
    grad_attn = wide_right("td,tc->dc", attended, grad_middle)
    grad_attended = wide_left("tc,dc->td", grad_middle, attn_w)
    grad_attended = grad_attended.astype(jnp.bfloat16).reshape(images, local_seq, HEADS, HDIM)
    score_scale = 1.0 / math.sqrt(HDIM)
    probs_exact = jnp.exp(attention_scores(query, all_keys) - log_total)
    attn_probs = probs_exact.astype(jnp.bfloat16)
    grad_probs = jnp.einsum(
        "isha,itha->ihst", grad_attended, all_values, preferred_element_type=jnp.float32
    )
    grad_scores = probs_exact * (grad_probs - jnp.sum(grad_probs * probs_exact, -1, keepdims=True))
    grad_scores = grad_scores.astype(jnp.bfloat16)
    grad_query = (
        jnp.einsum("ihst,itha->isha", grad_scores, all_keys, preferred_element_type=jnp.float32)
        * score_scale
    )
    key_part = (
        jnp.einsum("ihst,isha->itha", grad_scores, query, preferred_element_type=jnp.float32)
        * score_scale
    )
    value_part = jnp.einsum(
        "ihst,isha->itha", attn_probs, grad_attended, preferred_element_type=jnp.float32
    )
    grad_key, grad_value = (
        lax.psum_scatter(
            key_part.astype(jnp.bfloat16), "shard", scatter_dimension=1, tiled=True
        ).astype(jnp.float32),
        lax.psum_scatter(
            value_part.astype(jnp.bfloat16), "shard", scatter_dimension=1, tiled=True
        ).astype(jnp.float32),
    )
    grad_projected = jnp.concatenate(
        [
            grad_query.reshape(token_count, model_width),
            grad_key.reshape(token_count, model_width),
            grad_value.reshape(token_count, model_width),
        ],
        1,
    ).astype(jnp.bfloat16)
    grad_qkv = jnp.einsum("td,tc->dc", normed_a, grad_projected, preferred_element_type=jnp.float32)
    grad_normed_a = jnp.einsum(
        "tc,dc->td", grad_projected, qkv_w, preferred_element_type=jnp.float32
    )
    _, first_back = jax.vjp(layer_norm, token_rows, gain_a.astype(jnp.float32))
    grad_rows_norm, grad_gain_a = first_back(grad_normed_a)
    grad_block_in = (grad_middle + grad_rows_norm).reshape(grad_output.shape)
    return (
        grad_block_in,
        (grad_qkv, grad_attn, grad_gain_a, grad_gain_b, grad_router),
        (grad_expert_in, grad_expert_out),
    )


def reduce_weights(weight_grads):
    return (
        lax.psum_scatter(weight_grads[0], ("expert", "shard"), scatter_dimension=0, tiled=True),
        lax.psum_scatter(weight_grads[1], ("expert", "shard"), scatter_dimension=0, tiled=True),
        lax.psum_scatter(weight_grads[2], ("expert", "shard"), scatter_dimension=0, tiled=True),
        lax.psum_scatter(weight_grads[3], ("expert", "shard"), scatter_dimension=0, tiled=True),
        lax.psum_scatter(weight_grads[4], ("expert", "shard"), scatter_dimension=0, tiled=True),
    )


def add_trees(left_tree, right_tree):
    if left_tree is None:
        return right_tree
    return jax.tree.map(lambda left_leaf, right_leaf: left_leaf + right_leaf, left_tree, right_tree)


def local(inputs, cotangent, w_qkv, w_attn, gain_one, gain_two, router, w_in, w_out, routes):
    gathered = (
        lax.all_gather(w_qkv[0], "shard", axis=0, tiled=True),
        lax.all_gather(w_attn[0], "shard", axis=0, tiled=True),
        lax.all_gather(gain_one[0], "shard", axis=0, tiled=True),
        lax.all_gather(gain_two[0], "shard", axis=0, tiled=True),
        lax.all_gather(router[0], "shard", axis=0, tiled=True),
    )
    expert_in = w_in[0]
    expert_out = w_out[0]
    section_index = lax.axis_index("section")
    first_section = section_index == 0
    micro_count = inputs.shape[0]
    local_routes = routes[0, :, 0, 0]
    incoming = jnp.zeros(inputs.shape[1:], jnp.float32)
    outputs = jnp.zeros(inputs.shape, jnp.float32)
    kept_steps = []
    for step_index in range(micro_count + 1):
        early_micro = min(step_index, micro_count - 1)
        late_micro = max(step_index - 1, 0)
        micro_now = jnp.where(first_section, early_micro, late_micro)
        block_in = jnp.where(first_section, inputs[early_micro], incoming)
        result, kept_state = forward_block(
            block_in, gathered, expert_in, expert_out, local_routes[micro_now]
        )
        is_valid = jnp.where(first_section, step_index < micro_count, step_index >= 1)
        outputs = outputs.at[micro_now].set(jnp.where(is_valid, result, outputs[micro_now]))
        kept_steps.append(kept_state)
        if step_index < micro_count:
            incoming = from_behind(result.astype(jnp.bfloat16), "section", 1).astype(jnp.float32)
    kept_all = jax.tree.map(lambda *leaves: jnp.stack(leaves), *kept_steps)
    grads_in = jnp.zeros(inputs.shape, jnp.float32)
    back_incoming = jnp.zeros(inputs.shape[1:], jnp.float32)
    weight_total = None
    expert_total = None
    for step_index in range(micro_count + 1):
        early_micro = min(micro_count - step_index, micro_count - 1)
        late_micro = max(micro_count - 1 - step_index, 0)
        micro_now = jnp.where(first_section, early_micro, late_micro)
        is_valid = jnp.where(first_section, step_index >= 1, step_index < micro_count)
        seed_grad = jnp.where(is_valid, cotangent[late_micro], 0.0)
        grad_output = jnp.where(first_section, back_incoming, seed_grad)
        kept_state = jax.tree.map(lambda stacked: stacked[micro_now + section_index], kept_all)
        grad_block_in, weight_grads, expert_grads = backward_block(
            grad_output, kept_state, gathered, expert_in, expert_out
        )
        rounded = grad_block_in.astype(jnp.bfloat16)
        stored = jnp.where(first_section, grad_block_in, rounded.astype(jnp.float32))
        grads_in = grads_in.at[micro_now].set(jnp.where(is_valid, stored, grads_in[micro_now]))
        if step_index < micro_count:
            back_incoming = from_behind(rounded, "section", -1).astype(jnp.float32)
        expert_total = add_trees(expert_total, expert_grads)
        weight_total = add_trees(weight_total, reduce_weights(weight_grads))
    grad_qkv, grad_attn, grad_gain_a, grad_gain_b, grad_router = weight_total
    return (
        outputs[None],
        grads_in[None],
        grad_qkv[None],
        grad_attn[None],
        grad_gain_a[None],
        grad_gain_b[None],
        grad_router[None],
        expert_total[0][None],
        expert_total[1][None],
    )


def solution(mesh):
    return jax.shard_map(
        local,
        mesh=mesh,
        in_specs=(
            P(None, "expert", "shard", None),
            P(None, "expert", "shard", None),
            P("section", "shard", None),
            P("section", "shard", None),
            P("section", "shard"),
            P("section", "shard"),
            P("section", "shard", None),
            P("section", "expert", None, "shard"),
            P("section", "expert", "shard", None),
            P("section", None, "expert", "shard", None, None),
        ),
        out_specs=(
            P("section", None, "expert", "shard", None),
            P("section", None, "expert", "shard", None),
            P("section", ("expert", "shard"), None),
            P("section", ("expert", "shard"), None),
            P("section", ("expert", "shard")),
            P("section", ("expert", "shard")),
            P("section", ("expert", "shard"), None),
            P("section", "expert", None, "shard"),
            P("section", "expert", "shard", None),
        ),
        check_vma=False,
    )
```

profile of v0, /device:TPU:16, one launch (start us, length us, event | category | flops | bytes accessed | tf_op | source)
XLA Modules:
  0.0 1614.0 jit_solution(18037383775875775742)
XLA Ops:
  17.1 11.8 all-reduce.13
  29.0 14.2 all-gather.4
  43.5 14.8 all-gather.8.cloned.1.call-done
  63.7 18.6 %all_gather.54 = bf16[1,256,12,64]{3,2,0,1:T(8,128)(2,1)S(1)} all-gather(bf16[1,64,12,64]{3,2,0,1:T(8,128)(2,1)} %bitcast.1067), channel_id=1, replica_groups=mesh['section'=2,'expert'=16,'shard'=4] {'shard'}, dimensions={1}, use_global_device_ids=true | all-gather | bytes 491520 | tf_op jit(solution)/shard_map/all_gather | solution.py:79
  83.8 16.8 %all_gather.53 = bf16[1,256,12,64]{3,2,0,1:T(8,128)(2,1)} all-gather(bf16[1,64,12,64]{3,2,0,1:T(8,128)(2,1)} %bitcast.1066), channel_id=1, replica_groups=mesh['section'=2,'expert'=16,'shard'=4] {'shard'}, dimensions={1}, use_global_device_ids=true | all-gather | bytes 491520 | tf_op jit(solution)/shard_map/all_gather | solution.py:80
  113.7 14.0 all_to_all.198
  128.0 14.0 all_gather.58
  151.1 21.7 %reduce-scatter.31.cloned.1.call-done = bf16[2,80,768]{2,1,0:T(8,128)(2,1)} async-done(((bf16[2,320,768]{2,1,0:T(8,128)(2,1)}), bf16[2,80,768]{2,1,0:T(8,128)(2,1)}) %reduce-scatter.31.cloned.1.call-update) | async-done | bytes 245776 | tf_op jit(solution)/shard_map/reduce_scatter | solution.py:107
  174.6 7.6 all-to-all-start.1
  222.5 14.0 all_gather.60
  240.4 14.7 all_gather.59
  271.0 7.2 all-to-all-start.2
  286.4 14.1 all_gather.61
  378.7 15.2 all_gather.63
  402.3 15.6 all_gather.62
  438.2 7.2 all-to-all-start.4
  453.6 14.0 all_gather.64
  485.9 15.0 reduce-scatter.35.cloned.1.call-done
  502.7 7.3 all-to-all-start.5
  528.5 6.7 all-to-all-start.6
  543.4 14.8 all_gather.65
  559.2 6.7 fusion.61
  580.4 10.2 reduce-scatter.37.cloned.1.call-done
  592.4 7.2 all-to-all-start.7
  656.6 13.7 reduce-scatter.45.cloned.1.call-done
  690.9 7.2 all-to-all-start.8
  708.4 15.5 all_gather.66
  724.9 6.7 fusion.66
  749.4 6.8 reduce-scatter.39.cloned.1.call-done
  758.0 7.2 all-to-all-start.9
  819.5 16.3 %reduce-scatter.49.cloned.1.call-done = bf16[64,768]{1,0:T(8,128)(2,1)} async-done(((bf16[256,768]{1,0:T(8,128)(2,1)}), bf16[64,768]{1,0:T(8,128)(2,1)}) %reduce-scatter.49.cloned.1.call-update) | async-done | bytes 98320
  853.7 7.2 all-to-all-start.10
  871.2 15.7 all_gather.67
  887.9 6.7 fusion.71
  911.9 7.3 reduce-scatter.41.cloned.1.call-done
  921.0 7.3 all-to-all-start.11
  954.5 8.0 add_bitcast_fusion.1
  980.0 16.7 %reduce-scatter.53.cloned.1.call-done = bf16[64,768]{1,0:T(8,128)(2,1)} async-done(((bf16[256,768]{1,0:T(8,128)(2,1)}), bf16[64,768]{1,0:T(8,128)(2,1)}) %reduce-scatter.53.cloned.1.call-update) | async-done | bytes 98320
  998.1 9.1 add_add_fusion
  1007.2 191.0 %fusion.523 = (f32[16,2304]{1,0:T(8,128)}, f32[16,768]{1,0:T(8,128)}, f32[16,32]{1,0:T(8,128)S(1)}) fusion(f32[768,2304]{1,0:T(8,128)} %add_add_fusion, f32[768,768]{1,0:T(8,128)} %add_add_fusion.1, f32[768,32]{1,0:T(8,128)S(1)} %copy-done.82), kind=kCustom, calls=%all-reduce-scatter.3 | all-reduce-scatter fusion | flops 3178497 | bytes 9734656
  1200.5 14.6 collective-permute-start.49
  1221.6 7.9 add_bitcast_fusion
  1307.4 160.7 %all-reduce.12 = (f32[768]{0:T(1024)}, f32[768]{0:T(1024)}) all-reduce(f32[768]{0:T(1024)S(1)} %add_add_fusion.12, f32[768]{0:T(1024)S(1)} %add_add_fusion.11), channel_id=31, replica_groups=mesh['section'=2,'expert'=16,'shard'=4] {'expert','shard'}, use_global_device_ids=true, to_apply=%region_113.114.clone | all-reduce | flops 1536 | bytes 12288
  1470.1 24.5 %collective-permute-start.17 = (f32[16,2304]{1,0:T(8,128)}, f32[16,2304]{1,0:T(8,128)S(1)}, u32[]{:S(2)}, u32[]{:S(2)}) collective-permute-start(f32[16,2304]{1,0:T(8,128)} %get-tuple-element.188), channel_id=1, source_target_pairs={{0,14},{1,15},{2,16},{3,17},{4,18},{5,19},{6,20},{7,21},{8,22},{9,... | collective-permute-start | bytes 442376
  1504.0 8.0 collective-permute-start.12
  1524.4 12.3 concatenate.32
  1551.2 25.0 %concatenate.31 = f32[268,768]{1,0:T(8,128)} concatenate(f32[12,768]{1,0:T(8,128)} %copy-done.131, f32[16,768]{1,0:T(8,128)} %copy-done.130, f32[16,768]{1,0:T(8,128)} %copy-done.132, f32[16,768]{1,0:T(8,128)} %copy-done.133, f32[16,768]{1,0:T(8,128)} %copy-done.134, f32[16,768]{1,0:T(8,128)} %copy-done.135, f32[16,768]{1,0:T(8,128)} %copy-done.136, f32[16,768]{1,0:T(8,128)} %copy-done.137, ...), dimensions={0} | concatenate | bytes 1646592
  1577.7 27.8 %concatenate.30 = f32[268,2304]{1,0:T(8,128)} concatenate(f32[12,2304]{1,0:T(8,128)S(1)} %collective-permute-done.19, f32[16,2304]{1,0:T(8,128)S(1)} %collective-permute-done.18, f32[16,2304]{1,0:T(8,128)S(1)} %collective-permute-done.17, f32[16,2304]{1,0:T(8,128)S(1)} %collective-permute-done.16, f32[16,2304]{1,0:T(8,128)S(1)} %copy-done.122, f32[16,2304]{1,0:T(8,128)S(1)} %copy-done.124, ...), dimensions={0} | concatenate | bytes 4939776
  (1008 shorter events, 667.1 us)
Async XLA Ops:
  7.3 51.0 %all-gather.8.cloned.1.call-start = ((), (), s32[]{:S(2)}) async-start(), calls=%async_computation.30 | async-start | bytes 4423680 | tf_op jit(solution)/shard_map/all_gather | solution.py:265
  8.0 98.0 %all-gather.10.cloned.1.call-start = ((), (), s32[]{:S(2)}) async-start(), calls=%async_computation.31 | async-start | bytes 1474560 | tf_op jit(solution)/shard_map/all_gather | solution.py:266
  8.7 164.0 %reduce-scatter.31.cloned.1.call-start = ((), (), s32[]{:S(2)}) async-start(), calls=%async_computation.24 | async-start | bytes 1228800 | tf_op jit(solution)/shard_map/reduce_scatter | solution.py:107
  174.6 25.1 %all-to-all-start.1 = ((bf16[2,80,768]{2,0,1:T(2,128)(2,1)}), bf16[2,80,768]{2,0,1:T(2,128)(2,1)}, u32[]{:S(2)}, u32[]{:S(2)}) async-start(bf16[2,80,768]{2,0,1:T(2,128)(2,1)} %copy.463), calls=%async_computation.2 | async-start | bytes 491520 | tf_op jit(solution)/shard_map/all_to_all | solution.py:110
  278.3 54.7 %reduce-scatter.33.cloned.1.call-start = ((), (), s32[]{:S(2)}) async-start(), calls=%async_computation.25 | async-start | bytes 1228800 | tf_op jit(solution)/shard_map/reduce_scatter | solution.py:107
  445.5 55.4 %reduce-scatter.35.cloned.1.call-start = ((), (), s32[]{:S(2)}) async-start(), calls=%async_computation.26 | async-start | bytes 1228800 | tf_op jit(solution)/shard_map/reduce_scatter | solution.py:107
  535.2 55.4 %reduce-scatter.37.cloned.1.call-start = ((), (), s32[]{:S(2)}) async-start(), calls=%async_computation.27 | async-start | bytes 1228800 | tf_op jit(solution)/shard_map/reduce_scatter | solution.py:185
  599.6 53.4 %reduce-scatter.43.cloned.1.call-start = ((), (), s32[]{:S(2)}) async-start(), calls=%async_computation.32 | async-start | bytes 491520
  627.1 43.2 %reduce-scatter.45.cloned.1.call-start = ((), (), s32[]{:S(2)}) async-start(), calls=%async_computation.33 | async-start | bytes 491520
  690.9 16.2 %all-to-all-start.8 = ((bf16[32,5,768]{2,1,0:T(8,128)(2,1)}), bf16[32,5,768]{2,1,0:T(8,128)(2,1)}, u32[]{:S(2)}, u32[]{:S(2)}) async-start(bf16[32,5,768]{2,1,0:T(8,128)(2,1)} %reshape.1771), calls=%async_computation.12 | async-start | bytes 786432 | tf_op jit(solution)/shard_map/all_to_all | solution.py:170
  698.1 58.1 %reduce-scatter.39.cloned.1.call-start = ((), (), s32[]{:S(2)}) async-start(), calls=%async_computation.28 | async-start | bytes 1228800 | tf_op jit(solution)/shard_map/reduce_scatter | solution.py:185
  765.2 50.6 %reduce-scatter.47.cloned.1.call-start = ((), (), s32[]{:S(2)}) async-start(), calls=%async_computation.34 | async-start | bytes 491520
  792.7 43.1 %reduce-scatter.49.cloned.1.call-start = ((), (), s32[]{:S(2)}) async-start(), calls=%async_computation.35 | async-start | bytes 491520
  853.7 16.2 %all-to-all-start.10 = ((bf16[32,5,768]{2,1,0:T(8,128)(2,1)}), bf16[32,5,768]{2,1,0:T(8,128)(2,1)}, u32[]{:S(2)}, u32[]{:S(2)}) async-start(bf16[32,5,768]{2,1,0:T(8,128)(2,1)} %reshape.1782), calls=%async_computation.15 | async-start | bytes 786432 | tf_op jit(solution)/shard_map/all_to_all | solution.py:170
  860.9 58.3 %reduce-scatter.41.cloned.1.call-start = ((), (), s32[]{:S(2)}) async-start(), calls=%async_computation.29 | async-start | bytes 1228800 | tf_op jit(solution)/shard_map/reduce_scatter | solution.py:185
  928.3 50.3 %reduce-scatter.51.cloned.1.call-start = ((), (), s32[]{:S(2)}) async-start(), calls=%async_computation.36 | async-start | bytes 491520
  954.2 42.5 %reduce-scatter.53.cloned.1.call-start = ((), (), s32[]{:S(2)}) async-start(), calls=%async_computation.37 | async-start | bytes 491520
  1198.3 37.0 %collective-permute-start.50 = (f32[16,32]{1,0:T(8,128)S(1)}, f32[16,32]{1,0:T(8,128)S(1)}, u32[]{:S(2)}, u32[]{:S(2)}) collective-permute-start(f32[16,32]{1,0:T(8,128)S(1)} %get-tuple-element.190), channel_id=1, source_target_pairs={{0,15},{1,16},{2,17},{3,18},{4,19},{5,20},{6,21},{7,22},{8,23},{9,... | collective-permute-start | bytes 6152
  1200.5 36.8 %collective-permute-start.49 = (f32[16,32]{1,0:T(8,128)S(1)}, f32[16,32]{1,0:T(8,128)S(1)}, u32[]{:S(2)}, u32[]{:S(2)}) collective-permute-start(f32[16,32]{1,0:T(8,128)S(1)} %get-tuple-element.190), channel_id=1, source_target_pairs={{0,14},{1,15},{2,16},{3,17},{4,18},{5,19},{6,20},{7,21},{8,22},{9,... | collective-permute-start | bytes 6152
  1215.1 18.2 %collective-permute-start.51 = (f32[12,32]{1,0:T(8,128)S(1)}, f32[12,32]{1,0:T(8,128)S(1)}, u32[]{:S(2)}, u32[]{:S(2)}) collective-permute-start(f32[12,32]{1,0:T(8,128)S(1)} %slice.215), channel_id=1, source_target_pairs={{0,16},{1,17},{2,18},{3,19},{4,20},{5,21},{6,22},{7,23},{8,24},{9,... | collective-permute-start | bytes 4616
  1240.1 15.4 collective-permute-start.43
  1243.4 16.5 %collective-permute-start.42 = (f32[16,32]{1,0:T(8,128)S(1)}, f32[16,32]{1,0:T(8,128)S(1)}, u32[]{:S(2)}, u32[]{:S(2)}) collective-permute-start(f32[16,32]{1,0:T(8,128)S(1)} %get-tuple-element.190), channel_id=1, source_target_pairs={{0,7},{1,8},{2,9},{3,10},{4,11},{5,12},{6,13},{7,14},{8,15},{9,16}... | collective-permute-start | bytes 6152
  1246.3 15.8 collective-permute-start.41
  1248.5 16.1 collective-permute-start.40
  1251.1 15.5 collective-permute-start.39
  1264.6 16.1 collective-permute-start.34
  1268.6 14.4 collective-permute-start.33
  1270.5 14.4 collective-permute-start.32
  1293.7 174.5 %collective-permute-start.23 = (f32[16,768]{1,0:T(8,128)}, f32[16,768]{1,0:T(8,128)}, u32[]{:S(2)}, u32[]{:S(2)}) collective-permute-start(f32[16,768]{1,0:T(8,128)} %get-tuple-element.189), channel_id=1, source_target_pairs={{0,4},{1,5},{2,6},{3,7},{4,8},{5,9},{6,10},{7,11},{8,12},{9,13},{1... | collective-permute-start | bytes 147464
  1295.6 174.5 %collective-permute-start.22 = (f32[16,768]{1,0:T(8,128)}, f32[16,768]{1,0:T(8,128)}, u32[]{:S(2)}, u32[]{:S(2)}) collective-permute-start(f32[16,768]{1,0:T(8,128)} %get-tuple-element.189), channel_id=1, source_target_pairs={{0,3},{1,4},{2,5},{3,6},{4,7},{5,8},{6,9},{7,10},{8,11},{9,12},{10... | collective-permute-start | bytes 147464
  1300.1 194.5 %collective-permute-start.21 = (f32[16,768]{1,0:T(8,128)}, f32[16,768]{1,0:T(8,128)}, u32[]{:S(2)}, u32[]{:S(2)}) collective-permute-start(f32[16,768]{1,0:T(8,128)} %get-tuple-element.189), channel_id=1, source_target_pairs={{0,2},{1,3},{2,4},{3,5},{4,6},{5,7},{6,8},{7,9},{8,10},{9,11},{10,... | collective-permute-start | bytes 147464
  1302.1 194.5 %collective-permute-start.20 = (f32[16,768]{1,0:T(8,128)}, f32[16,768]{1,0:T(8,128)}, u32[]{:S(2)}, u32[]{:S(2)}) collective-permute-start(f32[16,768]{1,0:T(8,128)} %get-tuple-element.189), channel_id=1, source_target_pairs={{0,1},{1,2},{2,3},{3,4},{4,5},{5,6},{6,7},{7,8},{8,9},{9,10},{10,1... | collective-permute-start | bytes 147464
  1304.9 193.6 %collective-permute-start.19 = (f32[12,2304]{1,0:T(8,128)}, f32[12,2304]{1,0:T(8,128)S(1)}, u32[]{:S(2)}, u32[]{:S(2)}) collective-permute-start(f32[12,2304]{1,0:T(8,128)} %slice.213), channel_id=1, source_target_pairs={{0,16},{1,17},{2,18},{3,19},{4,20},{5,21},{6,22},{7,23},{8,24},{9,... | collective-permute-start | bytes 331784
  1468.1 34.0 %collective-permute-start.18 = (f32[16,2304]{1,0:T(8,128)}, f32[16,2304]{1,0:T(8,128)S(1)}, u32[]{:S(2)}, u32[]{:S(2)}) collective-permute-start(f32[16,2304]{1,0:T(8,128)} %get-tuple-element.188), channel_id=1, source_target_pairs={{0,15},{1,16},{2,17},{3,18},{4,19},{5,20},{6,21},{7,22},{8,23},{9,... | collective-permute-start | bytes 442376
  1470.1 34.0 %collective-permute-start.17 = (f32[16,2304]{1,0:T(8,128)}, f32[16,2304]{1,0:T(8,128)S(1)}, u32[]{:S(2)}, u32[]{:S(2)}) collective-permute-start(f32[16,2304]{1,0:T(8,128)} %get-tuple-element.188), channel_id=1, source_target_pairs={{0,14},{1,15},{2,16},{3,17},{4,18},{5,19},{6,20},{7,21},{8,22},{9,... | collective-permute-start | bytes 442376
  1494.6 17.5 %collective-permute-start.16 = (f32[16,2304]{1,0:T(8,128)}, f32[16,2304]{1,0:T(8,128)S(1)}, u32[]{:S(2)}, u32[]{:S(2)}) collective-permute-start(f32[16,2304]{1,0:T(8,128)} %get-tuple-element.188), channel_id=1, source_target_pairs={{0,13},{1,14},{2,15},{3,16},{4,17},{5,18},{6,19},{7,20},{8,21},{9,... | collective-permute-start | bytes 442376
  1496.5 18.7 %collective-permute-start.15 = (f32[16,2304]{1,0:T(8,128)}, f32[16,2304]{1,0:T(8,128)S(1)}, u32[]{:S(2)}, u32[]{:S(2)}) collective-permute-start(f32[16,2304]{1,0:T(8,128)} %get-tuple-element.188), channel_id=1, source_target_pairs={{0,12},{1,13},{2,14},{3,15},{4,16},{5,17},{6,18},{7,19},{8,20},{9,... | collective-permute-start | bytes 442376
  1498.5 19.7 %collective-permute-start.14 = (f32[16,2304]{1,0:T(8,128)}, f32[16,2304]{1,0:T(8,128)S(1)}, u32[]{:S(2)}, u32[]{:S(2)}) collective-permute-start(f32[16,2304]{1,0:T(8,128)} %get-tuple-element.188), channel_id=1, source_target_pairs={{0,11},{1,12},{2,13},{3,14},{4,15},{5,16},{6,17},{7,18},{8,19},{9,... | collective-permute-start | bytes 442376
  1502.1 34.6 %collective-permute-start.13 = (f32[16,2304]{1,0:T(8,128)}, f32[16,2304]{1,0:T(8,128)}, u32[]{:S(2)}, u32[]{:S(2)}) collective-permute-start(f32[16,2304]{1,0:T(8,128)} %get-tuple-element.188), channel_id=1, source_target_pairs={{0,10},{1,11},{2,12},{3,13},{4,14},{5,15},{6,16},{7,17},{8,18},{9,... | collective-permute-start | bytes 442376
  1504.0 34.7 %collective-permute-start.12 = (f32[16,2304]{1,0:T(8,128)}, f32[16,2304]{1,0:T(8,128)}, u32[]{:S(2)}, u32[]{:S(2)}) collective-permute-start(f32[16,2304]{1,0:T(8,128)} %get-tuple-element.188), channel_id=1, source_target_pairs={{0,9},{1,10},{2,11},{3,12},{4,13},{5,14},{6,15},{7,16},{8,17},{9,1... | collective-permute-start | bytes 442376
  1512.1 28.6 %collective-permute-start.11 = (f32[16,2304]{1,0:T(8,128)}, f32[16,2304]{1,0:T(8,128)}, u32[]{:S(2)}, u32[]{:S(2)}) collective-permute-start(f32[16,2304]{1,0:T(8,128)} %get-tuple-element.188), channel_id=1, source_target_pairs={{0,8},{1,9},{2,10},{3,11},{4,12},{5,13},{6,14},{7,15},{8,16},{9,17... | collective-permute-start | bytes 442376
  1515.3 30.6 %collective-permute-start.10 = (f32[16,2304]{1,0:T(8,128)}, f32[16,2304]{1,0:T(8,128)}, u32[]{:S(2)}, u32[]{:S(2)}) collective-permute-start(f32[16,2304]{1,0:T(8,128)} %get-tuple-element.188), channel_id=1, source_target_pairs={{0,7},{1,8},{2,9},{3,10},{4,11},{5,12},{6,13},{7,14},{8,15},{9,16}... | collective-permute-start | bytes 442376
  1518.2 29.6 %collective-permute-start.9 = (f32[16,2304]{1,0:T(8,128)}, f32[16,2304]{1,0:T(8,128)}, u32[]{:S(2)}, u32[]{:S(2)}) collective-permute-start(f32[16,2304]{1,0:T(8,128)} %get-tuple-element.188), channel_id=1, source_target_pairs={{0,6},{1,7},{2,8},{3,9},{4,10},{5,11},{6,12},{7,13},{8,14},{9,15},... | collective-permute-start | bytes 442376
  1536.8 40.9 %collective-permute-start.8 = (f32[16,2304]{1,0:T(8,128)S(1)}, f32[16,2304]{1,0:T(8,128)}, u32[]{:S(2)}, u32[]{:S(2)}) collective-permute-start(f32[16,2304]{1,0:T(8,128)S(1)} %copy-done.91), channel_id=1, source_target_pairs={{0,5},{1,6},{2,7},{3,8},{4,9},{5,10},{6,11},{7,12},{8,13},{9,14},{... | collective-permute-start | bytes 442376
  1538.7 39.0 %collective-permute-start.7 = (f32[16,2304]{1,0:T(8,128)S(1)}, f32[16,2304]{1,0:T(8,128)}, u32[]{:S(2)}, u32[]{:S(2)}) collective-permute-start(f32[16,2304]{1,0:T(8,128)S(1)} %copy-done.91), channel_id=1, source_target_pairs={{0,4},{1,5},{2,6},{3,7},{4,8},{5,9},{6,10},{7,11},{8,12},{9,13},{1... | collective-permute-start | bytes 442376
  1540.6 37.1 %collective-permute-start.6 = (f32[16,2304]{1,0:T(8,128)S(1)}, f32[16,2304]{1,0:T(8,128)}, u32[]{:S(2)}, u32[]{:S(2)}) collective-permute-start(f32[16,2304]{1,0:T(8,128)S(1)} %copy-done.91), channel_id=1, source_target_pairs={{0,3},{1,4},{2,5},{3,6},{4,7},{5,8},{6,9},{7,10},{8,11},{9,12},{10... | collective-permute-start | bytes 442376
  1545.8 31.9 %collective-permute-start.5 = (f32[16,2304]{1,0:T(8,128)S(1)}, f32[16,2304]{1,0:T(8,128)}, u32[]{:S(2)}, u32[]{:S(2)}) collective-permute-start(f32[16,2304]{1,0:T(8,128)S(1)} %copy-done.91), channel_id=1, source_target_pairs={{0,2},{1,3},{2,4},{3,5},{4,6},{5,7},{6,8},{7,9},{8,10},{9,11},{10,... | collective-permute-start | bytes 442376
  1547.8 29.9 %collective-permute-start.4 = (f32[16,2304]{1,0:T(8,128)S(1)}, f32[16,2304]{1,0:T(8,128)}, u32[]{:S(2)}, u32[]{:S(2)}) collective-permute-start(f32[16,2304]{1,0:T(8,128)S(1)} %copy-done.91), channel_id=1, source_target_pairs={{0,1},{1,2},{2,3},{3,4},{4,5},{5,6},{6,7},{7,8},{8,9},{9,10},{10,1... | collective-permute-start | bytes 442376
  (265 other events, 3949.8 us)
Sparse Core Ops, SparseCore 0:
  9.8 48.4 all-gather.7
  59.9 26.7 all-gather.9
  151.0 21.7 reduce-scatter.30
  309.4 22.6 reduce-scatter.32
  476.5 24.2 reduce-scatter.34
  568.9 21.5 reduce-scatter.36
  627.2 19.1 reduce-scatter.42
  649.5 20.7 reduce-scatter.44
  734.6 21.5 reduce-scatter.38
  792.8 19.1 reduce-scatter.46
  815.1 20.7 reduce-scatter.48
  897.7 21.4 reduce-scatter.40
  954.3 19.2 reduce-scatter.50
  976.0 20.7 reduce-scatter.52
where the time goes:
time: 1640 us; the launch traced here: 1610 us
  blocking collectives  575 us (35%)
  local copies, waits for them, and re-layouts  281 us (17%)
  starting transfers between devices  245 us (15%)
  matrix products  227 us (14%)
  waiting for transfers between devices  159 us (10%)
  other arithmetic  108 us (7%)
  between operations  19.9 us (1%)
    unnamed x3, blocking collectives  364 us
    unnamed x54, starting transfers between devices  160 us
    unnamed x521, local copies, waits for them, and re-layouts  157 us
    unnamed x68, waiting for transfers between devices  50.8 us
    all_gather x3, blocking collectives, forward_block(): lax.all_gather(key_local, 'shard', axis=1, tiled=True)  47.8 us
    all_gather x3, blocking collectives, forward_block(): lax.all_gather(value_local, 'shard', axis=1, tiled=True)  47.2 us
    all_gather x3, blocking collectives, backward_block(): slot_grads = lax.all_gather(arriving, 'shard', axis=1, tiled=True)  46.1 us
    another operation x19, other arithmetic, local(): kept_all = jax.tree.map(lambda *leaves: jnp.stack(leaves), *kept_steps)  44.3 us
  transfers between devices with their start and end apart: 77, of which 19 were waited for; matrix products, arithmetic and copies ran while one was open for 18% of the time, Pallas kernels for 0%

commit v1 on v0

v1 whole, which is shorter than its diff:
```python
import functools
import math

import jax
import jax.numpy as jnp
from jax import lax
from jax.experimental import pallas as pl
from jax.experimental.pallas import tpu as pltpu
from jax.sharding import PartitionSpec as P

F32 = jnp.float32
BF16 = jnp.bfloat16
D = 768
HEADS_OWN = 3
HDIM = 64
T = 64
CAP = 5
CHUNKS = 6
ROWS = 2 * CAP
N_EXPERT = 16
N_SHARD = 4
N_ALL = N_EXPERT * N_SHARD
SIDE = 64
BLOCK = N_EXPERT * SIDE
GROUP = N_EXPERT * CAP
ORDERED = CHUNKS * 2 * GROUP
EPS = 1e-06
SCALE = 1.0 / math.sqrt(HDIM)


def dot(a, b):
    return lax.dot_general(a, b, (((1,), (0,)), ((), ())), preferred_element_type=F32)


def dot_nt(a, b):
    return lax.dot_general(a, b, (((1,), (1,)), ((), ())), preferred_element_type=F32)


def dot_tn(a, b):
    return lax.dot_general(a, b, (((0,), (0,)), ((), ())), preferred_element_type=F32)


def iota(shape, dim):
    return lax.broadcasted_iota(jnp.int32, shape, dim)


def call(body, outs, ins, scratch=(), anywhere=(), scalars=1):
    specs = []
    for place in range(len(ins)):
        if place < scalars:
            specs.append(pl.BlockSpec(memory_space=pltpu.SMEM))
        elif place in anywhere:
            specs.append(pl.BlockSpec(memory_space=pl.ANY))
        else:
            specs.append(pl.BlockSpec(memory_space=pltpu.VMEM))
    return pl.pallas_call(
        body,
        out_shape=tuple(jax.ShapeDtypeStruct(shape, kind) for shape, kind in outs),
        in_specs=specs,
        out_specs=tuple(pl.BlockSpec(memory_space=pltpu.VMEM) for _ in outs),
        scratch_shapes=list(scratch),
        compiler_params=pltpu.CompilerParams(vmem_limit_bytes=48 * 1024 * 1024),
    )(*ins)


def fetch(mine, own, other, target, sem):
    @pl.when(mine)
    def _():
        pltpu.make_async_copy(own, target, sem).start()

    @pl.when(jnp.logical_not(mine))
    def _():
        pltpu.make_async_copy(other, target, sem).start()


def arrive(own, target, sem):
    pltpu.make_async_copy(own, target, sem).wait()


def norm_parts(rows):
    centered = rows - jnp.mean(rows, -1, keepdims=True)
    inverse = lax.rsqrt(jnp.mean(centered * centered, -1, keepdims=True) + EPS)
    return centered * inverse, inverse


def norm_back(grad, gain, unit, inverse):
    scaled = grad * gain
    return inverse * (
        scaled
        - jnp.mean(scaled, -1, keepdims=True)
        - unit * jnp.mean(scaled * unit, -1, keepdims=True)
    )


def split_pair(values):
    upper = values.astype(BF16)
    return upper, (values - upper.astype(F32)).astype(BF16)


def slots_in_row(route_row):
    named = (iota((32, 2 * T), 0) == route_row).astype(F32)
    earlier = ((iota((2 * T, 2 * T), 0) & (T - 1)) < (iota((2 * T, 2 * T), 1) & (T - 1))).astype(BF16)
    before = dot(named.astype(BF16), earlier)
    return route_row * CAP + jnp.sum(before * named, 0, keepdims=True).astype(jnp.int32)


def slots_in_column(route_column):
    named = (iota((2 * T, 32), 1) == route_column).astype(F32)
    earlier = ((iota((2 * T, 2 * T), 1) & (T - 1)) < (iota((2 * T, 2 * T), 0) & (T - 1))).astype(BF16)
    before = dot(earlier, named.astype(BF16))
    return route_column * CAP + jnp.sum(before * named, 1, keepdims=True).astype(jnp.int32)


def packed_place(index):
    within = index & (SIDE - 1)
    chunk = (within * 205) >> 11
    return (index >> 6) * ROWS + within - chunk * ROWS, chunk


def to_packed(slot_row, rows):
    slot, chunk = packed_place(iota((BLOCK, 2 * T), 0))
    hit = slot == slot_row
    total = None
    for c in range(CHUNKS):
        mask = jnp.where(hit & (chunk == c), 1.0, 0.0).astype(BF16)
        part = dot(mask, rows[:, c * 128 : (c + 1) * 128])
        total = part if total is None else total + part
    return total.astype(BF16)


def from_packed(slot_column, packed):
    slot, chunk = packed_place(iota((2 * T, BLOCK), 1))
    hit = slot == slot_column
    parts = []
    for c in range(CHUNKS):
        mask = jnp.where(hit & (chunk == c), 1.0, 0.0).astype(BF16)
        parts.append(dot(mask, packed))
    return jnp.concatenate(parts, 1)


def send_to_holders(packed, out_ref):
    blocks = packed.reshape(N_EXPERT, SIDE, 128)
    for s in range(N_SHARD):
        out_ref[:, s] = blocks


def sum_of_holders(in_ref):
    total = in_ref[:, 0].astype(F32)
    for s in range(1, N_SHARD):
        total = total + in_ref[:, s].astype(F32)
    return total.astype(BF16).reshape(BLOCK, 128)


def order_rows(order, packed_ref, store):
    for pair in range(2):
        low, high = 2 * pair * BLOCK, (2 * pair + 1) * BLOCK
        both = jnp.concatenate(
            [packed_ref[low : low + BLOCK, :], packed_ref[high : high + BLOCK, :]], 1
        )
        ordered = dot(order, both).astype(BF16)
        for half in range(2):
            group = 2 * pair + half
            for c in range(CHUNKS):
                for j in range(2):
                    start = c * 2 * GROUP + j * GROUP
                    store(j, group, c, ordered[start : start + GROUP, half * 128 : half * 128 + 128])


def unorder_rows(back_order, staged_ref, out_ref):
    for pair in range(2):
        both = jnp.concatenate([staged_ref[2 * pair], staged_ref[2 * pair + 1]], 1)
        packed = dot(back_order, both).astype(BF16)
        low, high = 2 * pair * BLOCK, (2 * pair + 1) * BLOCK
        out_ref[low : low + BLOCK, :] = packed[:, :128]
        out_ref[high : high + BLOCK, :] = packed[:, 128:]


def stage_rows(j, rows, staged_ref):
    for group in range(N_SHARD):
        for c in range(CHUNKS):
            start = c * 2 * GROUP + j * GROUP
            staged_ref[group, start : start + GROUP, :] = rows[
                group * GROUP : (group + 1) * GROUP, c * 128 : (c + 1) * 128
            ]


def head_mask(h):
    lane = iota((1, 256), 1)
    return ((lane >= h * HDIM) & (lane < (h + 1) * HDIM)).astype(BF16)


def pack_weights(ids, w, out):
    me = ids[1]
    for s in range(N_SHARD):
        place = (s - me) & (N_SHARD - 1)
        for j in range(3):
            piece = w[:, j * D + s * 192 : j * D + s * 192 + 192]
            out[place, :, j * 256 : j * 256 + 256] = jnp.concatenate(
                [piece, jnp.zeros((192, 64), BF16)], 1
            )


def join_weights(ids, p0, p1, p2, p3, out):
    me = ids[1]
    for k, piece in enumerate((p0, p1, p2, p3)):
        out[(me - k) & (N_SHARD - 1)] = piece[...]


def join_small(ids, p0, p1, p2, p3, out, held):
    mine, me = ids[0], ids[1]
    for k, piece in enumerate((p0, p1, p2, p3)):
        for o in range(2):
            section = mine if o == 0 else 1 - mine
            held[section, (me - k) & (N_SHARD - 1)] = piece[o]
    out[...] = jnp.zeros(out.shape, BF16)
    for section in range(2):
        for a in range(N_SHARD):
            out[section, 64:128, a * 192 : (a + 1) * 192] = held[section, a]


def first_norm(section, ids, h, small, out):
    unit, _ = norm_parts(h[...])
    out[...] = (unit * small[section, 96:97, :].astype(F32)).astype(BF16)


def attention(section, ids, x0, x1, x2, x3, own_w, other_w, own_a, other_a, o0, o1, o2, o3, kept, projected, w, a, sems):
    mine = ids[0] == section
    fetch(mine, own_w, other_w, w, sems.at[0])
    fetch(mine, own_a, other_a, a, sems.at[1])
    x = jnp.concatenate([x0[...], x1[...], x2[...], x3[...]], 0)
    kept[:, :D] = x
    arrive(own_w, w, sems.at[0])
    whole = dot(x, w[...].reshape(D, D)).astype(BF16)
    projected[...] = whole
    query, key, value = whole[:, :256], whole[:, 256:512], whole[:, 512:]
    attended = None
    for h in range(HEADS_OWN):
        mask = head_mask(h)
        scores = dot_nt(query * mask, key) * SCALE
        raised = jnp.exp(scores - jnp.max(scores, -1, keepdims=True))
        probs = (raised / jnp.sum(raised, -1, keepdims=True)).astype(BF16)
        part = dot(probs, value * mask)
        attended = part if attended is None else attended + part
    attended = attended.astype(BF16)
    kept[:, D:] = attended
    arrive(own_a, a, sems.at[1])
    result = dot(attended[:, :192], a[...]).astype(BF16)
    for k, out in enumerate((o0, o1, o2, o3)):
        out[...] = result[k * T : (k + 1) * T, :]


def dispatch(section, ids, h, o0, o1, o2, o3, small, route_row, route_column, out, middle_out, normed_out, gates_out):
    middle = h[...] + (
        (o0[...].astype(F32) + o1[...].astype(F32)) + (o2[...].astype(F32) + o3[...].astype(F32))
    )
    middle_out[...] = middle
    unit, _ = norm_parts(middle)
    normed = (unit * small[section, 97:98, :].astype(F32)).astype(BF16)
    normed_out[...] = normed
    packed = to_packed(slots_in_row(route_row[...]), jnp.concatenate([normed, normed], 0))
    send_to_holders(packed, out)
    logits = dot_nt(normed, small[section])
    logits = jnp.concatenate([logits, logits], 0)
    named = iota((2 * T, 128), 1) == route_column[...] + 64
    chosen = jnp.sum(jnp.where(named, logits, 0.0), 1, keepdims=True)
    one, two = chosen[:T], chosen[T:]
    top = jnp.maximum(one, two)
    one, two = jnp.exp(one - top), jnp.exp(two - top)
    total = one + two
    gates_out[0] = jnp.broadcast_to(one / total, (T, 128))
    gates_out[1] = jnp.broadcast_to(two / total, (T, 128))


def expert_forward(section, ids, arrived, order, back_order, own_in, other_in, own_out, other_out, out, kept, slope, w_in, w_out, staged, sems):
    mine = ids[0] == section
    for j in range(2):
        fetch(mine, own_in.at[j], other_in.at[j], w_in.at[j], sems.at[0, j])
        fetch(mine, own_out.at[j], other_out.at[j], w_out.at[j], sems.at[1, j])

    def store(j, group, c, rows):
        kept[0, j, group * GROUP : (group + 1) * GROUP, c * 128 : (c + 1) * 128] = rows

    order_rows(order[...], arrived, store)
    for j in range(2):
        arrive(own_in.at[j], w_in.at[j], sems.at[0, j])
        up = dot(kept[0, j], w_in[j])
        share = 0.5 * (1.0 + lax.erf(up * math.sqrt(0.5)))
        hidden = (up * share).astype(BF16)
        kept[1, j] = hidden
        slope[j] = (share + up * jnp.exp(-0.5 * up * up) * (1.0 / math.sqrt(2.0 * math.pi))).astype(BF16)
        arrive(own_out.at[j], w_out.at[j], sems.at[1, j])
        stage_rows(j, dot(hidden, w_out[j]).astype(BF16), staged)
    unorder_rows(back_order[...], staged, out)


def combined(returned, gates, route_column, taken, middle):
    rows = from_packed(slots_in_column(route_column[...]), sum_of_holders(returned))
    taken[...] = rows.astype(BF16)
    return middle[...] + gates[0][:, :1] * rows[:T] + gates[1][:, :1] * rows[T:]


def combine_next(ids, returned, gates, route_column, middle, small, result, taken, h, normed):
    value = combined(returned, gates, route_column, taken, middle)
    result[...] = value
    rounded = value.astype(BF16).astype(F32)
    h[...] = rounded
    unit, _ = norm_parts(rounded)
    normed[...] = (unit * small[1, 96:97, :].astype(F32)).astype(BF16)


def gate_backward(section, grad, gates, taken, route_row, route_column, small, out, grad_logits, part):
    first, second = gates[0][:, :1], gates[1][:, :1]
    rows = jnp.concatenate([(grad * first).astype(BF16), (grad * second).astype(BF16)], 0)
    send_to_holders(to_packed(slots_in_row(route_row[...]), rows), out)
    gate_one = jnp.sum(grad * taken[:T, :].astype(F32), 1, keepdims=True)
    gate_two = jnp.sum(grad * taken[T:, :].astype(F32), 1, keepdims=True)
    mean = first * gate_one + second * gate_two
    lanes = iota((T, 128), 1) - 64
    column = route_column[...]
    logits = jnp.where(lanes == column[:T], first * (gate_one - mean), 0.0) + jnp.where(
        lanes == column[T:], second * (gate_two - mean), 0.0
    )
    upper, lower = split_pair(logits)
    grad_logits[0] = upper
    grad_logits[1] = lower
    part[...] = dot(upper, small[section]) + dot(lower, small[section])


def start_backward(section, ids, grad, gates, taken, route_row, route_column, small, out, grad_logits, part):
    gate_backward(section, grad[...], gates, taken, route_row, route_column, small, out, grad_logits, part)


def expert_backward(section, ids, arrived, order, back_order, slope, own_in, other_in, own_out, other_out, out, kept, w_in, w_out, staged, sems):
    mine = ids[0] == section
    for j in range(2):
        fetch(mine, own_out.at[j], other_out.at[j], w_out.at[j], sems.at[1, j])
        fetch(mine, own_in.at[j], other_in.at[j], w_in.at[j], sems.at[0, j])

    def store(j, group, c, rows):
        kept[0, j, group * GROUP : (group + 1) * GROUP, c * 128 : (c + 1) * 128] = rows

    order_rows(order[...], arrived, store)
    for j in range(2):
        arrive(own_out.at[j], w_out.at[j], sems.at[1, j])
        grad_up = (dot_nt(kept[0, j], w_out[j]) * slope[j].astype(F32)).astype(BF16)
        kept[1, j] = grad_up
        arrive(own_in.at[j], w_in.at[j], sems.at[0, j])
        stage_rows(j, dot_nt(grad_up, w_in[j]).astype(BF16), staged)
    unorder_rows(back_order[...], staged, out)


def middle_backward(section, ids, returned, route_column, grad, part, middle, normed, grad_logits, small, grad_middle, sent, routed):
    rows = from_packed(slots_in_column(route_column[...]), sum_of_holders(returned))
    grad_normed = part[...] + rows[:T] + rows[T:]
    unit, inverse = norm_parts(middle[...])
    value = grad[...] + norm_back(grad_normed, small[section, 97:98, :].astype(F32), unit, inverse)
    grad_middle[...] = value
    sent[...] = value.astype(BF16)
    upper, lower = split_pair(jnp.sum(grad_normed * unit, 0, keepdims=True))
    routed[:T, :D] = normed[...]
    routed[:T, D : D + 128] = grad_logits[0]
    routed[:T, D + 128 :] = grad_logits[1]
    place = iota((16, D), 0)
    routed[T:, :D] = jnp.where(place == 0, upper, jnp.where(place == 1, lower, 0.0)).astype(BF16)
    named = (iota((16, 128), 1) == 97) & (iota((16, 128), 0) < 2)
    routed[T:, D : D + 128] = jnp.where(named, 1.0, 0.0).astype(BF16)
    routed[T:, D + 128 :] = jnp.zeros((16, 128), BF16)


def attention_backward(section, ids, g0, g1, g2, g3, kept, projected, small, own_w, other_w, own_a, other_a, n0, n1, n2, n3, packed, w, a, sems):
    mine = ids[0] == section
    fetch(mine, own_w, other_w, w, sems.at[0])
    fetch(mine, own_a, other_a, a.at[pl.ds(0, 192), :], sems.at[1])
    a[192:, :] = jnp.zeros((64, D), BF16)
    grad = jnp.concatenate([g0[...], g1[...], g2[...], g3[...]], 0)
    packed[:256, D:] = grad
    arrive(own_a, a.at[pl.ds(0, 192), :], sems.at[1])
    grad_attended = dot_nt(grad, a[...]).astype(BF16)
    query, key, value = projected[:, :256], projected[:, 256:512], projected[:, 512:]
    grad_query, grad_key, grad_value = None, None, None
    for h in range(HEADS_OWN):
        mask = head_mask(h)
        query_part, grad_part = query * mask, grad_attended * mask
        scores = dot_nt(query_part, key) * SCALE
        raised = jnp.exp(scores - jnp.max(scores, -1, keepdims=True))
        probs = raised / jnp.sum(raised, -1, keepdims=True)
        grad_probs = dot_nt(grad_part, value)
        grad_scores = probs * (grad_probs - jnp.sum(grad_probs * probs, -1, keepdims=True))
        grad_scores = grad_scores.astype(BF16)
        parts = (
            dot(grad_scores, key * mask),
            dot_tn(grad_scores, query_part),
            dot_tn(probs.astype(BF16), grad_part),
        )
        if h == 0:
            grad_query, grad_key, grad_value = parts
        else:
            grad_query, grad_key, grad_value = (
                grad_query + parts[0],
                grad_key + parts[1],
                grad_value + parts[2],
            )
    grad_projected = jnp.concatenate([grad_query * SCALE, grad_key * SCALE, grad_value], 1).astype(BF16)
    packed[:256, :D] = grad_projected
    arrive(own_w, w, sems.at[0])
    grad_normed = dot_nt(grad_projected, w[...].reshape(D, D))
    gain = jnp.sum(grad_normed * kept[:, :D].astype(F32), 0, keepdims=True)
    upper, lower = split_pair(gain / small[section, 96:97, :].astype(F32))
    place = iota((16, D), 0)
    packed[256:, :D] = jnp.where(place == 0, upper, jnp.where(place == 1, lower, 0.0)).astype(BF16)
    named = (iota((16, D), 1) == 96) & (iota((16, D), 0) < 2)
    packed[256:, D:] = jnp.where(named, 1.0, 0.0).astype(BF16)
    result = grad_normed.astype(BF16)
    for k, out in enumerate((n0, n1, n2, n3)):
        out[...] = result[k * T : (k + 1) * T, :]


def input_grad(section, n0, n1, n2, n3, h, grad_middle, small):
    grad_normed = (n0[...].astype(F32) + n1[...].astype(F32)) + (n2[...].astype(F32) + n3[...].astype(F32))
    unit, inverse = norm_parts(h[...])
    return grad_middle[...] + norm_back(grad_normed, small[section, 96:97, :].astype(F32), unit, inverse)


def input_backward_next(ids, n0, n1, n2, n3, h, grad_middle, small, gates, taken, route_row, route_column, grad_out, out, grad_logits, part):
    grad = input_grad(1, n0, n1, n2, n3, h, grad_middle, small).astype(BF16).astype(F32)
    grad_out[...] = grad
    gate_backward(0, grad, gates, taken, route_row, route_column, small, out, grad_logits, part)


def input_backward_last(ids, n0, n1, n2, n3, h, grad_middle, small, grad_out):
    grad_out[...] = input_grad(0, n0, n1, n2, n3, h, grad_middle, small)


def expert_weight_grads(ids, f0, f1, rf0, rf1, b0, b1, rb0, rb1, grad_in, grad_out, fwd, bwd, sems):
    j = pl.program_id(0)
    mine = ids[0] == 0
    fetch(mine, f0.at[:, j], f1.at[:, j], fwd.at[0], sems.at[0])
    fetch(mine, rf0.at[:, j], rf1.at[:, j], fwd.at[1], sems.at[1])
    fetch(mine, b0.at[:, j], b1.at[:, j], bwd.at[0], sems.at[2])
    fetch(mine, rb0.at[:, j], rb1.at[:, j], bwd.at[1], sems.at[3])
    arrive(f0.at[:, j], fwd.at[0], sems.at[0])
    arrive(rf0.at[:, j], fwd.at[1], sems.at[1])
    arrive(b0.at[:, j], bwd.at[0], sems.at[2])
    arrive(rb0.at[:, j], bwd.at[1], sems.at[3])
    grad_in[0] = dot_tn(fwd[0, 0], bwd[0, 1]) + dot_tn(fwd[1, 0], bwd[1, 1])
    grad_out[0] = dot_tn(fwd[0, 1], bwd[0, 0]) + dot_tn(fwd[1, 1], bwd[1, 0])


def shared_weight_grads(ids, k0, k1, rk0, rk1, p0, p1, rp0, rp1, r0, r1, rr0, rr1, out, kept, packed, routed, sems):
    mine = ids[0] == 0
    copies = (
        (k0, k1, kept.at[0]),
        (rk0, rk1, kept.at[1]),
        (p0, p1, packed.at[0]),
        (rp0, rp1, packed.at[1]),
        (r0, r1, routed.at[0]),
        (rr0, rr1, routed.at[1]),
    )
    for n, (own, other, target) in enumerate(copies):
        fetch(mine, own, other, target, sems.at[n])
    for n, (own, other, target) in enumerate(copies):
        arrive(own, target, sems.at[n])
    grad_qkv = dot_tn(kept[0, :, :D], packed[0, :256, :D]) + dot_tn(kept[1, :, :D], packed[1, :256, :D])
    grad_attn = dot_tn(kept[0, :, D:], packed[0, :256, D:]) + dot_tn(kept[1, :, D:], packed[1, :256, D:])
    extra = None
    for m in range(2):
        rows = routed[m, :, :D]
        part = (
            dot_tn(rows, routed[m, :, D : D + 128])
            + dot_tn(rows, routed[m, :, D + 128 :])
            + dot_tn(packed[m, 256:, :D], packed[m, 256:, D : D + 128])
        )
        extra = part if extra is None else extra + part
    middle = grad_qkv[:, 128:256] + extra
    out[:, :48, :128] = grad_qkv[:, :128].astype(BF16).reshape(N_EXPERT, 48, 128)
    out[:, :48, 128:256] = middle.astype(BF16).reshape(N_EXPERT, 48, 128)
    out[:, :48, 256:] = grad_qkv[:, 256:].astype(BF16).reshape(N_EXPERT, 48, 512)
    row, column = iota((256, 256), 0), iota((256, 256), 1)
    spread = ((row & 15) < 12) & (column == (row >> 4) * 12 + (row & 15))
    spread = jnp.where(spread, 1.0, 0.0).astype(BF16)
    out[:, 48:, :] = dot(spread, grad_attn.astype(BF16)).astype(BF16).reshape(N_EXPERT, 16, D)


def sum_shared(ids, arrived, out, attn, total):
    me = ids[1]
    summed = arrived[0].astype(F32)
    for n in range(1, N_EXPERT):
        summed = summed + arrived[n].astype(F32)
    total[...] = summed
    for s in range(N_SHARD):
        out[(s - me) & (N_SHARD - 1), :12, :] = total[s * 12 : s * 12 + 12, :]
    attn[...] = total[48:, :]


def place_shared(ids, q0, q1, q2, q3, qkv, extra, held):
    me = ids[1]
    for k, piece in enumerate((q0, q1, q2, q3)):
        held[(me - k) & (N_SHARD - 1)] = piece[...]
    total = None
    for a in range(N_SHARD):
        for j in range(3):
            qkv[:, j * D + a * 192 : j * D + a * 192 + 192] = held[a, :12, j * 256 : j * 256 + 192]
        part = held[a, :12, 128:256]
        total = part if total is None else total + part
    extra[...] = total


def along(value, axis, by):
    count = lax.axis_size(axis)
    return lax.ppermute(value, axis, [(i, (i + by) % count) for i in range(count)])


def gather_shards(value):
    return [value] + [along(value, "shard", k) for k in range(1, N_SHARD)]


def return_shards(pieces):
    return [pieces[0]] + [along(pieces[k], "shard", -k) for k in range(1, N_SHARD)]


def exchange(value):
    return lax.all_to_all(value, ("expert", "shard"), 0, 0, tiled=True)


def swap(value):
    return lax.ppermute(value, "section", [(0, 1), (1, 0)])


def up(value):
    return lax.ppermute(value, "section", [(0, 1)])


def down(value):
    return lax.ppermute(value, "section", [(1, 0)])


def dma(*shape):
    return pltpu.SemaphoreType.DMA(shape)


def local(inputs, cotangent, w_qkv, w_attn, gain_one, gain_two, router, w_in, w_out, routes):
    section = lax.axis_index("section")
    me = lax.axis_index("shard")
    first = section == 0
    ids = jnp.stack([section, me]).astype(jnp.int32)

    thin = jnp.concatenate(
        [router[0].T, gain_one, gain_two, jnp.zeros((30, router.shape[1]), BF16)], 0
    )
    thin = jnp.stack([thin, swap(thin)])
    small = call(
        join_small,
        [((2, 128, D), BF16)],
        [ids, *gather_shards(thin)],
        [pltpu.VMEM((2, N_SHARD, 64, 192), BF16)],
    )[0]
    pieces = call(pack_weights, [((N_SHARD, 192, D), BF16)], [ids, w_qkv[0]])[0]
    own_w = call(
        join_weights,
        [((N_SHARD, 192, D), BF16)],
        [ids, pieces[0], *[along(pieces[k], "shard", k) for k in range(1, N_SHARD)]],
    )[0]
    other_w = swap(own_w)
    own_a = w_attn[0]
    other_a = swap(own_a)
    own_in, own_out = w_in[0], w_out[0]
    other_in, other_out = swap(own_in), swap(own_out)
    weights = (own_w, other_w, own_a, other_a)
    experts = (own_in, other_in, own_out, other_out)

    local_routes = routes[0, :, 0, 0]
    own_routes = lax.dynamic_index_in_dim(local_routes, section, 0, False)
    other_routes = swap(lax.dynamic_index_in_dim(local_routes, 1 - section, 0, False))
    flat = [
        jnp.where(first, own_routes, other_routes).T.reshape(1, 2 * T),
        jnp.where(first, other_routes, own_routes).T.reshape(1, 2 * T),
    ]
    columns = [value.reshape(2 * T, 1) for value in flat]

    place = jnp.arange(ORDERED, dtype=jnp.int32)
    within = place % (2 * GROUP)
    source = (
        ((within % GROUP) // CAP) * SIDE
        + (place // (2 * GROUP)) * ROWS
        + (within // GROUP) * CAP
        + within % CAP
    )
    order = (source[:, None] == jnp.arange(BLOCK, dtype=jnp.int32)[None, :]).astype(BF16)
    back_order = (source[None, :] == jnp.arange(BLOCK, dtype=jnp.int32)[:, None]).astype(BF16)

    packed_shape = ((N_EXPERT, N_SHARD, SIDE, 128), BF16)
    rows_shape = ((T, D), BF16)
    wide_shape = ((T, D), F32)
    flat_shape = ((N_ALL * SIDE, 128), BF16)
    per_expert = N_SHARD * GROUP

    def crossed(value):
        return exchange(value.reshape(N_ALL, SIDE, 128))

    def forward_part(s, h, normed):
        o0, o1, o2, o3, kept, projected = call(
            functools.partial(attention, s),
            [rows_shape] * 4 + [((256, D + 256), BF16), ((256, D), BF16)],
            [ids, *gather_shards(normed), *weights],
            [pltpu.VMEM((N_SHARD, 192, D), BF16), pltpu.VMEM((192, D), BF16), dma(2)],
            anywhere=(5, 6, 7, 8),
        )
        sent, middle, normed_b, gates = call(
            functools.partial(dispatch, s),
            [packed_shape, wide_shape, rows_shape, ((2, T, 128), F32)],
            [ids, h, *return_shards([o0, o1, o2, o3]), small, flat[s], columns[s]],
        )
        arrived = crossed(sent).reshape(N_ALL * SIDE, 128)
        sent, expert_kept, slope = call(
            functools.partial(expert_forward, s),
            [flat_shape, ((2, 2, per_expert, D), BF16), ((2, per_expert, D), BF16)],
            [ids, arrived, order, back_order, *experts],
            [
                pltpu.VMEM((2, D, D), BF16),
                pltpu.VMEM((2, D, D), BF16),
                pltpu.VMEM((N_SHARD, ORDERED, 128), BF16),
                dma(2, 2),
            ],
            anywhere=(4, 5, 6, 7),
        )
        returned = crossed(sent).reshape(N_EXPERT, N_SHARD, SIDE, 128)
        return returned, (kept, projected, middle, normed_b, gates, expert_kept, slope)

    def backward_part(s, grad, arrived, part, grad_logits, h, state):
        kept, projected, middle, normed_b, gates, expert_kept, slope = state
        sent, expert_grads = call(
            functools.partial(expert_backward, s),
            [flat_shape, ((2, 2, per_expert, D), BF16)],
            [ids, arrived.reshape(N_ALL * SIDE, 128), order, back_order, slope, *experts],
            [
                pltpu.VMEM((2, D, D), BF16),
                pltpu.VMEM((2, D, D), BF16),
                pltpu.VMEM((N_SHARD, ORDERED, 128), BF16),
                dma(2, 2),
            ],
            anywhere=(5, 6, 7, 8),
        )
        returned = crossed(sent).reshape(N_EXPERT, N_SHARD, SIDE, 128)
        grad_middle, sent, routed = call(
            functools.partial(middle_backward, s),
            [wide_shape, rows_shape, ((T + 16, D + 256), BF16)],
            [ids, returned, columns[s], grad, part, middle, normed_b, grad_logits, small],
        )
        n0, n1, n2, n3, packed = call(
            functools.partial(attention_backward, s),
            [rows_shape] * 4 + [((256 + 16, 2 * D), BF16)],
            [ids, *gather_shards(sent), kept, projected, small, *weights],
            [pltpu.VMEM((N_SHARD, 192, D), BF16), pltpu.VMEM((256, D), BF16), dma(2)],
            anywhere=(8, 9, 10, 11),
        )
        return return_shards([n0, n1, n2, n3]), grad_middle, expert_grads, routed, packed

    h_one = lax.dynamic_index_in_dim(inputs, section, 0, False).reshape(T, D)
    normed = call(functools.partial(first_norm, 0), [rows_shape], [ids, h_one, small])[0]
    returned, state_one = forward_part(0, h_one, normed)
    result_one, taken_one, h_two, normed = call(
        combine_next,
        [wide_shape, ((2 * T, D), BF16), wide_shape, rows_shape],
        [ids, returned, state_one[4], columns[0], state_one[2], small],
    )
    returned, state_two = forward_part(1, h_two, normed)
    result_two, taken_two = call(
        combine_last,
        [wide_shape, ((2 * T, D), BF16)],
        [ids, returned, state_two[4], columns[1], state_two[2]],
    )

    logits_shape = ((2, T, 128), BF16)
    seed = lax.dynamic_index_in_dim(cotangent, section, 0, False).reshape(T, D)
    sent, grad_logits, part = call(
        functools.partial(start_backward, 1),
        [packed_shape, logits_shape, wide_shape],
        [ids, seed, state_two[4], taken_two, flat[1], columns[1], small],
    )
    pieces, grad_middle, expert_grads_two, routed_two, packed_two = backward_part(
        1, seed, crossed(sent), part, grad_logits, h_two, state_two
    )
    grad_two, sent, grad_logits, part = call(
        input_backward_next,
        [wide_shape, packed_shape, logits_shape, wide_shape],
        [ids, *pieces, h_two, grad_middle, small, state_one[4], taken_one, flat[0], columns[0]],
    )
    pieces, grad_middle, expert_grads_one, routed_one, packed_one = backward_part(
        0, grad_two, crossed(sent), part, grad_logits, h_one, state_one
    )

    payload = call(
        shared_weight_grads,
        [((N_EXPERT, 64, D), BF16)],
        [
            ids,
            state_one[0], state_two[0], down(state_one[0]), up(state_two[0]),
            packed_one, packed_two, down(packed_one), up(packed_two),
            routed_one, routed_two, down(routed_one), up(routed_two),
        ],
        [
            pltpu.VMEM((2, 256, D + 256), BF16),
            pltpu.VMEM((2, 256 + 16, 2 * D), BF16),
            pltpu.VMEM((2, T + 16, D + 256), BF16),
            dma(6),
        ],
        anywhere=tuple(range(1, 13)),
    )[0]
    summed = lax.all_to_all(payload, "expert", 0, 0, tiled=True)
    shares, attn = call(
        sum_shared,
        [((N_SHARD, 16, D), F32), ((16, D), F32)],
        [ids, summed],
        [pltpu.VMEM((64, D), F32)],
    )
    grad_qkv, extra = call(
        place_shared,
        [((12, 3 * D), F32), ((12, 128), F32)],
        [ids, shares[0], *[along(shares[k], "shard", k) for k in range(1, N_SHARD)]],
        [pltpu.VMEM((N_SHARD, 16, D), F32)],
    )
    pairs = [
        (e * N_SHARD + s, (N_SHARD * s + e // N_SHARD) * N_SHARD + e % N_SHARD)
        for e in range(N_EXPERT)
        for s in range(N_SHARD)
    ]
    grad_attn = lax.ppermute(attn, ("expert", "shard"), pairs)[:12]

    grad_one = call(
        input_backward_last, [wide_shape], [ids, *pieces, h_one, grad_middle, small]
    )[0]
    block = pl.BlockSpec(memory_space=pl.ANY)
    half = pl.BlockSpec((1, D, D), lambda j: (j, 0, 0))
    grad_in, grad_out = pl.pallas_call(
        expert_weight_grads,
        grid=(2,),
        out_shape=(jax.ShapeDtypeStruct((2, D, D), F32), jax.ShapeDtypeStruct((2, D, D), F32)),
        in_specs=[pl.BlockSpec(memory_space=pltpu.SMEM)] + [block] * 8,
        out_specs=(half, half),
        scratch_shapes=[
            pltpu.VMEM((2, 2, per_expert, D), BF16),
            pltpu.VMEM((2, 2, per_expert, D), BF16),
            dma(4),
        ],
        compiler_params=pltpu.CompilerParams(vmem_limit_bytes=48 * 1024 * 1024),
    )(
        ids,
        state_one[5], state_two[5], down(state_one[5]), up(state_two[5]),
        expert_grads_one, expert_grads_two, down(expert_grads_one), up(expert_grads_two),
    )

    def by_micro(one, two):
        return jnp.where(first, jnp.stack([one, down(one)]), jnp.stack([up(two), two])).reshape(
            1, 2, 1, T, D
        )

    return (
        by_micro(result_one, result_two),
        by_micro(grad_one, grad_two),
        grad_qkv[None],
        grad_attn[None],
        extra[:, 96][None],
        extra[:, 97][None],
        extra[:, 64:96][None],
        grad_in[None],
        grad_out[None],
    )


def combine_last(ids, returned, gates, route_column, middle, result, taken):
    result[...] = combined(returned, gates, route_column, taken, middle)


def solution(mesh):
    return jax.shard_map(
        local,
        mesh=mesh,
        in_specs=(
            P(None, "expert", "shard", None),
            P(None, "expert", "shard", None),
            P("section", "shard", None),
            P("section", "shard", None),
            P("section", "shard"),
            P("section", "shard"),
            P("section", "shard", None),
            P("section", "expert", None, "shard"),
            P("section", "expert", "shard", None),
            P("section", None, "expert", "shard", None, None),
        ),
        out_specs=(
            P("section", None, "expert", "shard", None),
            P("section", None, "expert", "shard", None),
            P("section", ("expert", "shard"), None),
            P("section", ("expert", "shard"), None),
            P("section", ("expert", "shard")),
            P("section", ("expert", "shard")),
            P("section", ("expert", "shard"), None),
            P("section", "expert", None, "shard"),
            P("section", "expert", "shard", None),
        ),
        check_vma=False,
    )
```

time: 1640 us -> 473 us (0.29); the launches traced: 1610 us -> 464 us
  blocking collectives: 575 us -> 98.6 us
  local copies, waits for them, and re-layouts: 281 us -> 44.3 us
  matrix products: 227 us -> 0 us
  starting transfers between devices: 245 us -> 112 us
  other arithmetic: 108 us -> 6.32 us
  Pallas kernels: 0 us -> 82.6 us
  waiting for transfers between devices: 159 us -> 118 us
  between operations: 19.9 us -> 1.79 us
    unnamed x3 -> x0, blocking collectives: 364 us -> none
    dot_general x99 -> x0, matrix products: 227 us -> none  [the longest x3 20.1 us: backward_block(): jnp.einsum('end,efd->enf', slot_grads, expert_out, preferred_element_type...]
    all_gather x13 -> x0, blocking collectives: 197 us -> none  [the longest x3 47.8 us: forward_block(): lax.all_gather(key_local, 'shard', axis=1, tiled=True)]
    unnamed x54 -> x0, starting transfers between devices: 160 us -> none
    unnamed x521 -> x177, local copies, waits for them, and re-layouts: 157 us -> 40 us
    ppermute x4 -> x54, waiting for transfers between devices: 0.01 us -> 87.6 us  [the longest x33 74.9 us: along(): lax.ppermute(value, axis, [(i, (i + by) % count) for i in range(count)])]
    all_to_all x1 -> x5, blocking collectives: 14 us -> 98.6 us  [exchange(): return lax.all_to_all(value, ('expert', 'shard'), 0, 0, tiled=True)]
    pallas_call x0 -> x25, Pallas kernels: none -> 82.6 us  [the longest x24 70.2 us: call(): pl.pallas_call(body, out_shape=tuple((jax.ShapeDtypeStruct(shape, kind) f...]
  transfers between devices with their start and end apart: 77 -> 58, of which waited for: 19 -> 36; matrix products, arithmetic and copies ran while one was open for 18% -> 2% of each run, Pallas kernels for 0% -> 7%
where the time goes in v1:
time: 473 us; the launch traced here: 464 us
  waiting for transfers between devices  118 us (25%)
  starting transfers between devices  112 us (24%)
  blocking collectives  98.6 us (21%)
  Pallas kernels  82.6 us (17%)
  local copies, waits for them, and re-layouts  44.3 us (9%)
  other arithmetic  6.32 us (1%)
    all_to_all x5, blocking collectives, exchange(): return lax.all_to_all(value, ('expert', 'shard'), 0, 0, tiled=True)  98.6 us
    ppermute x33, waiting for transfers between devices, along(): lax.ppermute(value, axis, [(i, (i + by) % count) for i in range(count)])  74.9 us
    pallas_call x24, Pallas kernels, call(): pl.pallas_call(body, out_shape=tuple((jax.ShapeDtypeStruct(shape, kind) f...  70.2 us
    ppermute x33, starting transfers between devices, along(): lax.ppermute(value, axis, [(i, (i + by) % count) for i in range(count)])  45.5 us
    unnamed x177, local copies, waits for them, and re-layouts  40 us
    all_to_all x3, waiting for transfers between devices, exchange(): return lax.all_to_all(value, ('expert', 'shard'), 0, 0, tiled=True)  30.8 us
    all_to_all x3, starting transfers between devices, exchange(): return lax.all_to_all(value, ('expert', 'shard'), 0, 0, tiled=True)  24.9 us
    ppermute x7, starting transfers between devices, up(): return lax.ppermute(value, 'section', [(0, 1)])  19.9 us
  transfers between devices with their start and end apart: 58, of which 36 were waited for; matrix products, arithmetic and copies ran while one was open for 2% of the time, Pallas kernels for 7%

profile of v1, /device:TPU:16, one launch (start us, length us, event | category | flops | bytes accessed | tf_op | source)
XLA Modules:
  0.0 463.9 jit_solution(12766513496225736543)
XLA Ops:
  4.8 3.6 collective-permute-start.8
  9.4 4.5 collective-permute-done.7.p1
  13.9 7.5 %collective-permute-done.8.p2 = bf16[192,768]{1,0:T(8,128)(2,1)S(1)} collective-permute-done((bf16[192,768]{1,0:T(8,128)(2,1)S(1)}, bf16[192,768]{1,0:T(8,128)(2,1)S(1)}, u32[]{:S(2)}, u32[]{:S(2)}) %collective-permute-start.8) | collective-permute-done | bytes 294944 | tf_op jit(solution)/shard_map/ppermute | solution.py:510
  23.4 2.5 collective-permute-done
  33.2 2.8 collective-permute-done.3.p3
  38.0 6.0 %collective-permute-done.4.x1 = bf16[64,768]{1,0:T(8,128)(2,1)S(1)} collective-permute-done((bf16[64,768]{1,0:T(8,128)(2,1)}, bf16[64,768]{1,0:T(8,128)(2,1)S(1)}, u32[]{:S(2)}, u32[]{:S(2)}) %collective-permute-start.4) | collective-permute-done | bytes 98336 | tf_op jit(solution)/shard_map/ppermute | solution.py:510
  45.2 5.9 %collective-permute-done.5.x2 = bf16[64,768]{1,0:T(8,128)(2,1)} collective-permute-done((bf16[64,768]{1,0:T(8,128)(2,1)}, bf16[64,768]{1,0:T(8,128)(2,1)}, u32[]{:S(2)}, u32[]{:S(2)}) %collective-permute-start.5) | collective-permute-done | bytes 98336 | tf_op jit(solution)/shard_map/ppermute | solution.py:510
  53.0 2.9 collective-permute-done.6.x3
  58.4 3.4 shard_map.173
  64.1 3.1 collective-permute-start.12
  82.7 8.8 %all-to-all-start = ((bf16[64,64,128]{2,1,0:T(8,128)(2,1)}), bf16[64,64,128]{2,1,0:T(8,128)(2,1)}, u32[]{:S(2)}, u32[]{:S(2)}) async-start(bf16[64,64,128]{2,1,0:T(8,128)(2,1)} %bitcast.88), calls=%async_computation | async-start | bytes 2097152 | tf_op jit(solution)/shard_map/all_to_all | solution.py:522
  95.4 12.2 %all-to-all-done = bf16[64,64,128]{2,1,0:T(8,128)(2,1)} async-done(((bf16[64,64,128]{2,1,0:T(8,128)(2,1)}), bf16[64,64,128]{2,1,0:T(8,128)(2,1)}, u32[]{:S(2)}, u32[]{:S(2)}) %all-to-all-start) | async-done | bytes 1048608 | tf_op jit(solution)/shard_map/all_to_all | solution.py:522
  107.6 7.9 %shard_map.175 = (bf16[4096,128]{1,0:T(8,128)(2,1)S(1)}, bf16[2,2,320,768]{3,2,1,0:T(8,128)(2,1)}, bf16[2,320,768]{2,1,0:T(8,128)(2,1)S(1)}) custom-call(s32[2]{0:T(128)S(1)} %pad_add_fusion.ids, bf16[4096,128]{1,0:T(8,128)(2,1)} %bitcast.17.arrived, bf16[960,1024]{1,0:T(8,128)(2,1)} %fusion.1.order, bf16[1024,960]{1,0:T(8,128)(2,1)} %fusion.back_order, ...), custom_call_target="tpu_custom_call" | custom-call | tf_op jit(solution)/shard_map/pallas_call | solution.py:56
  115.5 22.3 %all_to_all.45 = bf16[64,64,128]{2,1,0:T(8,128)(2,1)S(1)} all-to-all(bf16[64,64,128]{2,1,0:T(8,128)(2,1)S(1)} %bitcast.94), channel_id=1, replica_groups=mesh['section'=2,'expert'=16,'shard'=4] {'expert','shard'}, dimensions={0} | all-to-all | bytes 2097152 | tf_op jit(solution)/shard_map/all_to_all | solution.py:522
  149.3 3.0 shard_map.177
  154.5 2.7 collective-permute-start.22
  160.7 3.0 collective-permute-done.23.o2
  170.1 18.6 %all_to_all.46 = bf16[64,64,128]{2,1,0:T(8,128)(2,1)S(1)} all-to-all(bf16[64,64,128]{2,1,0:T(8,128)(2,1)S(1)} %bitcast.92), channel_id=1, replica_groups=mesh['section'=2,'expert'=16,'shard'=4] {'expert','shard'}, dimensions={0} | all-to-all | bytes 2097152 | tf_op jit(solution)/shard_map/all_to_all | solution.py:522
  188.7 8.2 %shard_map.179 = (bf16[4096,128]{1,0:T(8,128)(2,1)S(1)}, bf16[2,2,320,768]{3,2,1,0:T(8,128)(2,1)}, bf16[2,320,768]{2,1,0:T(8,128)(2,1)S(1)}) custom-call(s32[2]{0:T(128)S(1)} %pad_add_fusion.ids, bf16[4096,128]{1,0:T(8,128)(2,1)S(1)} %bitcast.84, bf16[960,1024]{1,0:T(8,128)(2,1)} %fusion.1.order, bf16[1024,960]{1,0:T(8,128)(2,1)} %fusion.back_order, ...), custom_call_target="tpu_custom_call" | custom-call | tf_op jit(solution)/shard_map/pallas_call | solution.py:56
  198.9 8.0 %all-to-all-start.3 = ((bf16[64,64,128]{2,1,0:T(8,128)(2,1)}), bf16[64,64,128]{2,1,0:T(8,128)(2,1)}, u32[]{:S(2)}, u32[]{:S(2)}) async-start(bf16[64,64,128]{2,1,0:T(8,128)(2,1)} %bitcast.91), calls=%async_computation.3 | async-start | bytes 2097152 | tf_op jit(solution)/shard_map/all_to_all | solution.py:522
  208.5 10.3 %all-to-all-done.3 = bf16[64,64,128]{2,1,0:T(8,128)(2,1)} async-done(((bf16[64,64,128]{2,1,0:T(8,128)(2,1)}), bf16[64,64,128]{2,1,0:T(8,128)(2,1)}, u32[]{:S(2)}, u32[]{:S(2)}) %all-to-all-start.3) | async-done | bytes 1048608 | tf_op jit(solution)/shard_map/all_to_all | solution.py:522
  226.1 19.0 %all_to_all.47 = bf16[64,64,128]{2,1,0:T(8,128)(2,1)S(1)} all-to-all(bf16[64,64,128]{2,1,0:T(8,128)(2,1)S(1)} %bitcast.93), channel_id=1, replica_groups=mesh['section'=2,'expert'=16,'shard'=4] {'expert','shard'}, dimensions={0} | all-to-all | bytes 2097152 | tf_op jit(solution)/shard_map/all_to_all | solution.py:522
  245.1 8.1 %shard_map.182 = (bf16[4096,128]{1,0:T(8,128)(2,1)S(1)}, bf16[2,2,320,768]{3,2,1,0:T(8,128)(2,1)}) custom-call(s32[2]{0:T(128)S(1)} %pad_add_fusion.ids, bf16[4096,128]{1,0:T(8,128)(2,1)S(1)} %bitcast.85, bf16[960,1024]{1,0:T(8,128)(2,1)} %fusion.1.order, bf16[1024,960]{1,0:T(8,128)(2,1)} %fusion.back_order, bf16[2,320,768]{2,1,0:T(8,128)(2,1)S(1)} %copy-done.23, ...), custom_call_target="tpu_custom_call" | custom-call | tf_op jit(solution)/shard_map/pallas_call | solution.py:56
  253.3 19.6 %all_to_all.48 = bf16[64,64,128]{2,1,0:T(8,128)(2,1)S(1)} all-to-all(bf16[64,64,128]{2,1,0:T(8,128)(2,1)S(1)} %bitcast.95), channel_id=1, replica_groups=mesh['section'=2,'expert'=16,'shard'=4] {'expert','shard'}, dimensions={0} | all-to-all | bytes 2097152 | tf_op jit(solution)/shard_map/all_to_all | solution.py:522
  282.1 2.7 collective-permute-done.28.g3
  284.8 3.2 shard_map.184
  289.0 2.4 collective-permute-start.29
  294.7 3.0 collective-permute-done.30.n2
  301.9 19.1 %all_to_all.49 = bf16[64,64,128]{2,1,0:T(8,128)(2,1)S(1)} all-to-all(bf16[64,64,128]{2,1,0:T(8,128)(2,1)S(1)} %bitcast.90), channel_id=1, replica_groups=mesh['section'=2,'expert'=16,'shard'=4] {'expert','shard'}, dimensions={0} | all-to-all | bytes 2097152 | tf_op jit(solution)/shard_map/all_to_all | solution.py:522
  321.1 8.1 %shard_map.186 = (bf16[4096,128]{1,0:T(8,128)(2,1)S(1)}, bf16[2,2,320,768]{3,2,1,0:T(8,128)(2,1)}) custom-call(s32[2]{0:T(128)S(1)} %pad_add_fusion.ids, bf16[4096,128]{1,0:T(8,128)(2,1)S(1)} %bitcast.83, bf16[960,1024]{1,0:T(8,128)(2,1)} %fusion.1.order, bf16[1024,960]{1,0:T(8,128)(2,1)} %fusion.back_order, bf16[2,320,768]{2,1,0:T(8,128)(2,1)S(1)} %copy-done.21, ...), custom_call_target="tpu_custom_call" | custom-call | tf_op jit(solution)/shard_map/pallas_call | solution.py:56
  330.2 8.2 %all-to-all-start.7 = ((bf16[64,64,128]{2,1,0:T(8,128)(2,1)}), bf16[64,64,128]{2,1,0:T(8,128)(2,1)}, u32[]{:S(2)}, u32[]{:S(2)}) async-start(bf16[64,64,128]{2,1,0:T(8,128)(2,1)} %bitcast.89), calls=%async_computation.7 | async-start | bytes 2097152 | tf_op jit(solution)/shard_map/all_to_all | solution.py:522
  341.8 8.4 %all-to-all-done.7 = bf16[64,64,128]{2,1,0:T(8,128)(2,1)} async-done(((bf16[64,64,128]{2,1,0:T(8,128)(2,1)}), bf16[64,64,128]{2,1,0:T(8,128)(2,1)}, u32[]{:S(2)}, u32[]{:S(2)}) %all-to-all-start.7) | async-done | bytes 1048608 | tf_op jit(solution)/shard_map/all_to_all | solution.py:522
  366.3 3.3 shard_map.188
  373.4 3.1 collective-permute-start.41
  377.9 4.3 collective-permute-start.45
  383.5 4.3 collective-permute-start.51
  387.8 2.6 collective-permute-start.53
  391.7 4.3 shard_map.190
  396.1 6.6 %all-to-all-start.8 = ((bf16[16,64,768]{2,1,0:T(8,128)(2,1)}), bf16[16,64,768]{2,1,0:T(8,128)(2,1)S(1)}, u32[]{:S(2)}, u32[]{:S(2)}) async-start(bf16[16,64,768]{2,1,0:T(8,128)(2,1)} %shard_map.190), calls=%async_computation.8 | async-start | bytes 3145728 | tf_op jit(solution)/shard_map/all_to_all | solution.py:709
  404.0 3.3 collective-permute-done.18
  410.4 2.7 collective-permute-start.35
  413.0 2.6 collective-permute-done.35.n1
  417.8 3.9 collective-permute-done.36.n2
  423.6 4.5 collective-permute-done.37.n3
  432.4 3.5 collective-permute-start.47
  437.2 12.4 %shard_map.193 = (f32[2,768,768]{2,1,0:T(8,128)}, f32[2,768,768]{2,1,0:T(8,128)}) custom-call(s32[2]{0:T(128)S(1)} %pad_add_fusion.ids, bf16[2,2,320,768]{3,2,1,0:T(8,128)(2,1)} %get-tuple-element.133.f0, bf16[2,2,320,768]{3,2,1,0:T(8,128)(2,1)} %get-tuple-element.134.f1, bf16[2,2,320,768]{3,2,1,0:T(8,128)(2,1)} %collective-permute-done.50.rf0, ...), custom_call_target="tpu_custom_call" | custom-call | tf_op jit(solution)/shard_map/pallas_call | solution.py:734
  449.5 4.8 %collective-permute-start.49 = (f32[16,768]{1,0:T(8,128)S(1)}, f32[16,768]{1,0:T(8,128)S(1)}, u32[]{:S(2)}, u32[]{:S(2)}) collective-permute-start(f32[16,768]{1,0:T(8,128)S(1)} %get-tuple-element.131), channel_id=1, source_target_pairs={{0,0},{1,16},{2,32},{3,48},{4,1},{5,17},{6,33},{7,49},{8,2},{9,18}... | collective-permute-start | bytes 147464 | tf_op jit(solution)/shard_map/ppermute | solution.py:727
  456.6 5.9 %collective-permute-done.49 = f32[16,768]{1,0:T(8,128)S(1)} collective-permute-done((f32[16,768]{1,0:T(8,128)S(1)}, f32[16,768]{1,0:T(8,128)S(1)}, u32[]{:S(2)}, u32[]{:S(2)}) %collective-permute-start.49) | collective-permute-done | bytes 49184 | tf_op jit(solution)/shard_map/ppermute | solution.py:727
  (298 shorter events, 141.2 us)
Async XLA Ops:
  2.8 11.1 %collective-permute-start.7 = (bf16[192,768]{1,0:T(8,128)(2,1)S(1)}, bf16[192,768]{1,0:T(8,128)(2,1)S(1)}, u32[]{:S(2)}, u32[]{:S(2)}) collective-permute-start(bf16[192,768]{1,0:T(8,128)(2,1)S(1)} %get-tuple-element.161), channel_id=1, source_target_pairs={{0,1},{1,2},{2,3},{3,0},{4,5},{5,6},{6,7},{7,4},{8,9},{9,10},{10,1... | collective-permute-start | bytes 884744 | tf_op jit(solution)/shard_map/ppermute | solution.py:510
  4.8 16.6 %collective-permute-start.8 = (bf16[192,768]{1,0:T(8,128)(2,1)S(1)}, bf16[192,768]{1,0:T(8,128)(2,1)S(1)}, u32[]{:S(2)}, u32[]{:S(2)}) collective-permute-start(bf16[192,768]{1,0:T(8,128)(2,1)S(1)} %get-tuple-element.160), channel_id=1, source_target_pairs={{0,2},{1,3},{2,0},{3,1},{4,6},{5,7},{6,4},{7,5},{8,10},{9,11},{10,... | collective-permute-start | bytes 884744 | tf_op jit(solution)/shard_map/ppermute | solution.py:510
  8.4 13.0 %collective-permute-start.9 = (bf16[192,768]{1,0:T(8,128)(2,1)S(1)}, bf16[192,768]{1,0:T(8,128)(2,1)S(1)}, u32[]{:S(2)}, u32[]{:S(2)}) collective-permute-start(bf16[192,768]{1,0:T(8,128)(2,1)S(1)} %get-tuple-element.159), channel_id=1, source_target_pairs={{0,3},{1,0},{2,1},{3,2},{4,7},{5,4},{6,5},{7,6},{8,11},{9,8},{10,9... | collective-permute-start | bytes 884744 | tf_op jit(solution)/shard_map/ppermute | solution.py:510
  22.1 34.6 %collective-permute-start.10 = (bf16[4,192,768]{2,1,0:T(8,128)(2,1)S(1)}, bf16[4,192,768]{2,1,0:T(8,128)(2,1)S(1)}, u32[]{:S(2)}, u32[]{:S(2)}) collective-permute-start(bf16[4,192,768]{2,1,0:T(8,128)(2,1)S(1)} %shard_map.172.own_w), channel_id=1, source_target_pairs={{0,64},{64,0},{1,65},{65,1},{2,66},{66,2},{3,67},{67,3},{4,68},{68... | collective-permute-start | bytes 3538952 | tf_op jit(solution)/shard_map/ppermute | solution.py:526
  22.2 73.2 %collective-permute-start.16 = (bf16[2,768,768]{2,1,0:T(8,128)(2,1)}, bf16[2,768,768]{2,1,0:T(8,128)(2,1)}, u32[]{:S(2)}, u32[]{:S(2)}) collective-permute-start(bf16[2,768,768]{2,1,0:T(8,128)(2,1)} %bitcast.18.own_in), channel_id=1, source_target_pairs={{0,64},{64,0},{1,65},{65,1},{2,66},{66,2},{3,67},{67,3},{4,68},{68... | collective-permute-start | bytes 7077896 | tf_op jit(solution)/shard_map/ppermute | solution.py:526
  22.7 72.7 %collective-permute-start.17 = (bf16[2,768,768]{2,1,0:T(8,128)(2,1)}, bf16[2,768,768]{2,1,0:T(8,128)(2,1)}, u32[]{:S(2)}, u32[]{:S(2)}) collective-permute-start(bf16[2,768,768]{2,1,0:T(8,128)(2,1)} %bitcast.19.own_out), channel_id=1, source_target_pairs={{0,64},{64,0},{1,65},{65,1},{2,66},{66,2},{3,67},{67,3},{4,68},{68... | collective-permute-start | bytes 7077896 | tf_op jit(solution)/shard_map/ppermute | solution.py:526
  25.9 5.8 %collective-permute-start.1 = (bf16[2,64,192]{2,1,0:T(8,128)(2,1)S(1)}, bf16[2,64,192]{2,1,0:T(8,128)(2,1)S(1)}, u32[]{:S(2)}, u32[]{:S(2)}) collective-permute-start(bf16[2,64,192]{2,1,0:T(8,128)(2,1)S(1)} %pad_maximum_fusion.p0), channel_id=1, source_target_pairs={{0,1},{1,2},{2,3},{3,0},{4,5},{5,6},{6,7},{7,4},{8,9},{9,10},{10,1... | collective-permute-start | bytes 147464 | tf_op jit(solution)/shard_map/ppermute | solution.py:510
  27.2 6.0 %collective-permute-start.2 = (bf16[2,64,192]{2,1,0:T(8,128)(2,1)S(1)}, bf16[2,64,192]{2,1,0:T(8,128)(2,1)S(1)}, u32[]{:S(2)}, u32[]{:S(2)}) collective-permute-start(bf16[2,64,192]{2,1,0:T(8,128)(2,1)S(1)} %pad_maximum_fusion.p0), channel_id=1, source_target_pairs={{0,2},{1,3},{2,0},{3,1},{4,6},{5,7},{6,4},{7,5},{8,10},{9,11},{10,... | collective-permute-start | bytes 147464 | tf_op jit(solution)/shard_map/ppermute | solution.py:510
  38.0 6.0 %collective-permute-start.4 = (bf16[64,768]{1,0:T(8,128)(2,1)}, bf16[64,768]{1,0:T(8,128)(2,1)S(1)}, u32[]{:S(2)}, u32[]{:S(2)}) collective-permute-start(bf16[64,768]{1,0:T(8,128)(2,1)} %shard_map.170.x0), channel_id=1, source_target_pairs={{0,1},{1,2},{2,3},{3,0},{4,5},{5,6},{6,7},{7,4},{8,9},{9,10},{10,1... | collective-permute-start | bytes 294920 | tf_op jit(solution)/shard_map/ppermute | solution.py:510
  38.0 18.6 %collective-permute-start.11 = (bf16[192,768]{1,0:T(8,128)(2,1)S(1)}, bf16[192,768]{1,0:T(8,128)(2,1)S(1)}, u32[]{:S(2)}, u32[]{:S(2)}) collective-permute-start(bf16[192,768]{1,0:T(8,128)(2,1)S(1)} %bitcast.78), channel_id=1, source_target_pairs={{0,64},{64,0},{1,65},{65,1},{2,66},{66,2},{3,67},{67,3},{4,68},{68... | collective-permute-start | bytes 884744 | tf_op jit(solution)/shard_map/ppermute | solution.py:526
  44.7 6.4 %collective-permute-start.5 = (bf16[64,768]{1,0:T(8,128)(2,1)}, bf16[64,768]{1,0:T(8,128)(2,1)}, u32[]{:S(2)}, u32[]{:S(2)}) collective-permute-start(bf16[64,768]{1,0:T(8,128)(2,1)} %shard_map.170.x0), channel_id=1, source_target_pairs={{0,2},{1,3},{2,0},{3,1},{4,6},{5,7},{6,4},{7,5},{8,10},{9,11},{10,... | collective-permute-start | bytes 294920 | tf_op jit(solution)/shard_map/ppermute | solution.py:510
  56.6 10.6 %collective-permute-start.15 = (s32[64,2]{0,1:T(2,128)S(1)}, s32[64,2]{0,1:T(2,128)S(1)}, u32[]{:S(2)}, u32[]{:S(2)}) collective-permute-start(s32[64,2]{0,1:T(2,128)S(1)} %dynamic-slice_bitcast_fusion.2), channel_id=1, source_target_pairs={{0,64},{64,0},{1,65},{65,1},{2,66},{66,2},{3,67},{67,3},{4,68},{68... | collective-permute-start | bytes 1544 | tf_op jit(solution)/shard_map/ppermute | solution.py:526
  64.1 8.2 %collective-permute-start.12 = (bf16[64,768]{1,0:T(8,128)(2,1)}, bf16[64,768]{1,0:T(8,128)(2,1)}, u32[]{:S(2)}, u32[]{:S(2)}) collective-permute-start(bf16[64,768]{1,0:T(8,128)(2,1)} %get-tuple-element.75), channel_id=1, source_target_pairs={{0,3},{1,0},{2,1},{3,2},{4,7},{5,4},{6,5},{7,6},{8,11},{9,8},{10,9... | collective-permute-start | bytes 294920 | tf_op jit(solution)/shard_map/ppermute | solution.py:510
  67.2 7.4 %collective-permute-start.13 = (bf16[64,768]{1,0:T(8,128)(2,1)}, bf16[64,768]{1,0:T(8,128)(2,1)}, u32[]{:S(2)}, u32[]{:S(2)}) collective-permute-start(bf16[64,768]{1,0:T(8,128)(2,1)} %get-tuple-element.76), channel_id=1, source_target_pairs={{0,2},{1,3},{2,0},{3,1},{4,6},{5,7},{6,4},{7,5},{8,10},{9,11},{10,... | collective-permute-start | bytes 294920 | tf_op jit(solution)/shard_map/ppermute | solution.py:510
  67.7 8.3 %collective-permute-start.14 = (bf16[64,768]{1,0:T(8,128)(2,1)}, bf16[64,768]{1,0:T(8,128)(2,1)}, u32[]{:S(2)}, u32[]{:S(2)}) collective-permute-start(bf16[64,768]{1,0:T(8,128)(2,1)} %get-tuple-element.77), channel_id=1, source_target_pairs={{0,1},{1,2},{2,3},{3,0},{4,5},{5,6},{6,7},{7,4},{8,9},{9,10},{10,1... | collective-permute-start | bytes 294920 | tf_op jit(solution)/shard_map/ppermute | solution.py:510
  82.7 24.9 %all-to-all-start = ((bf16[64,64,128]{2,1,0:T(8,128)(2,1)}), bf16[64,64,128]{2,1,0:T(8,128)(2,1)}, u32[]{:S(2)}, u32[]{:S(2)}) async-start(bf16[64,64,128]{2,1,0:T(8,128)(2,1)} %bitcast.88), calls=%async_computation | async-start | bytes 2097152 | tf_op jit(solution)/shard_map/all_to_all | solution.py:522
  141.6 5.8 %collective-permute-start.19 = (bf16[64,768]{1,0:T(8,128)(2,1)S(1)}, bf16[64,768]{1,0:T(8,128)(2,1)S(1)}, u32[]{:S(2)}, u32[]{:S(2)}) collective-permute-start(bf16[64,768]{1,0:T(8,128)(2,1)S(1)} %get-tuple-element.84.x0), channel_id=1, source_target_pairs={{0,1},{1,2},{2,3},{3,0},{4,5},{5,6},{6,7},{7,4},{8,9},{9,10},{10,1... | collective-permute-start | bytes 294920 | tf_op jit(solution)/shard_map/ppermute | solution.py:510
  142.3 6.1 %collective-permute-start.20 = (bf16[64,768]{1,0:T(8,128)(2,1)S(1)}, bf16[64,768]{1,0:T(8,128)(2,1)S(1)}, u32[]{:S(2)}, u32[]{:S(2)}) collective-permute-start(bf16[64,768]{1,0:T(8,128)(2,1)S(1)} %get-tuple-element.84.x0), channel_id=1, source_target_pairs={{0,2},{1,3},{2,0},{3,1},{4,6},{5,7},{6,4},{7,5},{8,10},{9,11},{10,... | collective-permute-start | bytes 294920 | tf_op jit(solution)/shard_map/ppermute | solution.py:510
  154.5 6.2 %collective-permute-start.22 = (bf16[64,768]{1,0:T(8,128)(2,1)}, bf16[64,768]{1,0:T(8,128)(2,1)}, u32[]{:S(2)}, u32[]{:S(2)}) collective-permute-start(bf16[64,768]{1,0:T(8,128)(2,1)} %get-tuple-element.86), channel_id=1, source_target_pairs={{0,3},{1,0},{2,1},{3,2},{4,7},{5,4},{6,5},{7,6},{8,11},{9,8},{10,9... | collective-permute-start | bytes 294920 | tf_op jit(solution)/shard_map/ppermute | solution.py:510
  157.2 6.5 %collective-permute-start.23 = (bf16[64,768]{1,0:T(8,128)(2,1)}, bf16[64,768]{1,0:T(8,128)(2,1)}, u32[]{:S(2)}, u32[]{:S(2)}) collective-permute-start(bf16[64,768]{1,0:T(8,128)(2,1)} %get-tuple-element.87), channel_id=1, source_target_pairs={{0,2},{1,3},{2,0},{3,1},{4,6},{5,7},{6,4},{7,5},{8,10},{9,11},{10,... | collective-permute-start | bytes 294920 | tf_op jit(solution)/shard_map/ppermute | solution.py:510
  157.6 7.1 %collective-permute-start.24 = (bf16[64,768]{1,0:T(8,128)(2,1)}, bf16[64,768]{1,0:T(8,128)(2,1)}, u32[]{:S(2)}, u32[]{:S(2)}) collective-permute-start(bf16[64,768]{1,0:T(8,128)(2,1)} %get-tuple-element.88), channel_id=1, source_target_pairs={{0,1},{1,2},{2,3},{3,0},{4,5},{5,6},{6,7},{7,4},{8,9},{9,10},{10,1... | collective-permute-start | bytes 294920 | tf_op jit(solution)/shard_map/ppermute | solution.py:510
  198.9 19.9 %all-to-all-start.3 = ((bf16[64,64,128]{2,1,0:T(8,128)(2,1)}), bf16[64,64,128]{2,1,0:T(8,128)(2,1)}, u32[]{:S(2)}, u32[]{:S(2)}) async-start(bf16[64,64,128]{2,1,0:T(8,128)(2,1)} %bitcast.91), calls=%async_computation.3 | async-start | bytes 2097152 | tf_op jit(solution)/shard_map/all_to_all | solution.py:522
  275.2 5.8 %collective-permute-start.26 = (bf16[64,768]{1,0:T(8,128)(2,1)S(1)}, bf16[64,768]{1,0:T(8,128)(2,1)S(1)}, u32[]{:S(2)}, u32[]{:S(2)}) collective-permute-start(bf16[64,768]{1,0:T(8,128)(2,1)S(1)} %get-tuple-element.101.g0), channel_id=1, source_target_pairs={{0,1},{1,2},{2,3},{3,0},{4,5},{5,6},{6,7},{7,4},{8,9},{9,10},{10,1... | collective-permute-start | bytes 294920 | tf_op jit(solution)/shard_map/ppermute | solution.py:510
  276.0 6.1 %collective-permute-start.27 = (bf16[64,768]{1,0:T(8,128)(2,1)S(1)}, bf16[64,768]{1,0:T(8,128)(2,1)S(1)}, u32[]{:S(2)}, u32[]{:S(2)}) collective-permute-start(bf16[64,768]{1,0:T(8,128)(2,1)S(1)} %get-tuple-element.101.g0), channel_id=1, source_target_pairs={{0,2},{1,3},{2,0},{3,1},{4,6},{5,7},{6,4},{7,5},{8,10},{9,11},{10,... | collective-permute-start | bytes 294920 | tf_op jit(solution)/shard_map/ppermute | solution.py:510
  277.9 6.9 %collective-permute-start.28 = (bf16[64,768]{1,0:T(8,128)(2,1)S(1)}, bf16[64,768]{1,0:T(8,128)(2,1)S(1)}, u32[]{:S(2)}, u32[]{:S(2)}) collective-permute-start(bf16[64,768]{1,0:T(8,128)(2,1)S(1)} %get-tuple-element.101.g0), channel_id=1, source_target_pairs={{0,3},{1,0},{2,1},{3,2},{4,7},{5,4},{6,5},{7,6},{8,11},{9,8},{10,9... | collective-permute-start | bytes 294920 | tf_op jit(solution)/shard_map/ppermute | solution.py:510
  289.0 5.6 %collective-permute-start.29 = (bf16[64,768]{1,0:T(8,128)(2,1)S(1)}, bf16[64,768]{1,0:T(8,128)(2,1)S(1)}, u32[]{:S(2)}, u32[]{:S(2)}) collective-permute-start(bf16[64,768]{1,0:T(8,128)(2,1)S(1)} %get-tuple-element.105), channel_id=1, source_target_pairs={{0,3},{1,0},{2,1},{3,2},{4,7},{5,4},{6,5},{7,6},{8,11},{9,8},{10,9... | collective-permute-start | bytes 294920 | tf_op jit(solution)/shard_map/ppermute | solution.py:510
  291.4 6.2 %collective-permute-start.30 = (bf16[64,768]{1,0:T(8,128)(2,1)S(1)}, bf16[64,768]{1,0:T(8,128)(2,1)S(1)}, u32[]{:S(2)}, u32[]{:S(2)}) collective-permute-start(bf16[64,768]{1,0:T(8,128)(2,1)S(1)} %get-tuple-element.106), channel_id=1, source_target_pairs={{0,2},{1,3},{2,0},{3,1},{4,6},{5,7},{6,4},{7,5},{8,10},{9,11},{10,... | collective-permute-start | bytes 294920 | tf_op jit(solution)/shard_map/ppermute | solution.py:510
  291.4 6.9 %collective-permute-start.31 = (bf16[64,768]{1,0:T(8,128)(2,1)S(1)}, bf16[64,768]{1,0:T(8,128)(2,1)S(1)}, u32[]{:S(2)}, u32[]{:S(2)}) collective-permute-start(bf16[64,768]{1,0:T(8,128)(2,1)S(1)} %get-tuple-element.107), channel_id=1, source_target_pairs={{0,1},{1,2},{2,3},{3,0},{4,5},{5,6},{6,7},{7,4},{8,9},{9,10},{10,1... | collective-permute-start | bytes 294920 | tf_op jit(solution)/shard_map/ppermute | solution.py:510
  330.2 20.1 %all-to-all-start.7 = ((bf16[64,64,128]{2,1,0:T(8,128)(2,1)}), bf16[64,64,128]{2,1,0:T(8,128)(2,1)}, u32[]{:S(2)}, u32[]{:S(2)}) async-start(bf16[64,64,128]{2,1,0:T(8,128)(2,1)} %bitcast.89), calls=%async_computation.7 | async-start | bytes 2097152 | tf_op jit(solution)/shard_map/all_to_all | solution.py:522
  338.3 49.5 %collective-permute-start.43 = (bf16[272,1536]{1,0:T(8,128)(2,1)}, bf16[272,1536]{1,0:T(8,128)(2,1)}, u32[]{:S(2)}, u32[]{:S(2)}) collective-permute-start(bf16[272,1536]{1,0:T(8,128)(2,1)} %copy-done.25), channel_id=1, source_target_pairs={{0,64},{1,65},{2,66},{3,67},{4,68},{5,69},{6,70},{7,71},{8,72},{9,... | collective-permute-start | bytes 2506760 | tf_op jit(solution)/shard_map/ppermute | solution.py:530
  340.5 37.3 %collective-permute-start.40 = (bf16[256,1024]{1,0:T(8,128)(2,1)}, bf16[256,1024]{1,0:T(8,128)(2,1)}, u32[]{:S(2)}, u32[]{:S(2)}) collective-permute-start(bf16[256,1024]{1,0:T(8,128)(2,1)} %copy-done.3), channel_id=1, source_target_pairs={{64,0},{65,1},{66,2},{67,3},{68,4},{69,5},{70,6},{71,7},{72,8},{73... | collective-permute-start | bytes 1572872 | tf_op jit(solution)/shard_map/ppermute | solution.py:534
  358.6 5.8 %collective-permute-start.32 = (bf16[64,768]{1,0:T(8,128)(2,1)S(1)}, bf16[64,768]{1,0:T(8,128)(2,1)S(1)}, u32[]{:S(2)}, u32[]{:S(2)}) collective-permute-start(bf16[64,768]{1,0:T(8,128)(2,1)S(1)} %get-tuple-element.117.g0), channel_id=1, source_target_pairs={{0,1},{1,2},{2,3},{3,0},{4,5},{5,6},{6,7},{7,4},{8,9},{9,10},{10,1... | collective-permute-start | bytes 294920 | tf_op jit(solution)/shard_map/ppermute | solution.py:510
  359.3 6.1 %collective-permute-start.33 = (bf16[64,768]{1,0:T(8,128)(2,1)S(1)}, bf16[64,768]{1,0:T(8,128)(2,1)S(1)}, u32[]{:S(2)}, u32[]{:S(2)}) collective-permute-start(bf16[64,768]{1,0:T(8,128)(2,1)S(1)} %get-tuple-element.117.g0), channel_id=1, source_target_pairs={{0,2},{1,3},{2,0},{3,1},{4,6},{5,7},{6,4},{7,5},{8,10},{9,11},{10,... | collective-permute-start | bytes 294920 | tf_op jit(solution)/shard_map/ppermute | solution.py:510
  372.1 19.6 %collective-permute-start.42 = (bf16[272,1536]{1,0:T(8,128)(2,1)S(1)}, bf16[272,1536]{1,0:T(8,128)(2,1)S(1)}, u32[]{:S(2)}, u32[]{:S(2)}) collective-permute-start(bf16[272,1536]{1,0:T(8,128)(2,1)S(1)} %get-tuple-element.125.p0), channel_id=1, source_target_pairs={{64,0},{65,1},{66,2},{67,3},{68,4},{69,5},{70,6},{71,7},{72,8},{73... | collective-permute-start | bytes 2506760 | tf_op jit(solution)/shard_map/ppermute | solution.py:534
  373.4 8.7 %collective-permute-start.41 = (bf16[256,1024]{1,0:T(8,128)(2,1)S(1)}, bf16[256,1024]{1,0:T(8,128)(2,1)S(1)}, u32[]{:S(2)}, u32[]{:S(2)}) collective-permute-start(bf16[256,1024]{1,0:T(8,128)(2,1)S(1)} %copy-done.7), channel_id=1, source_target_pairs={{0,64},{1,65},{2,66},{3,67},{4,68},{5,69},{6,70},{7,71},{8,72},{9,... | collective-permute-start | bytes 1572872 | tf_op jit(solution)/shard_map/ppermute | solution.py:530
  376.6 54.5 %collective-permute-start.50 = (bf16[2,2,320,768]{3,2,1,0:T(8,128)(2,1)}, bf16[2,2,320,768]{3,2,1,0:T(8,128)(2,1)}, u32[]{:S(2)}, u32[]{:S(2)}) collective-permute-start(bf16[2,2,320,768]{3,2,1,0:T(8,128)(2,1)} %get-tuple-element.133.f0), channel_id=1, source_target_pairs={{64,0},{65,1},{66,2},{67,3},{68,4},{69,5},{70,6},{71,7},{72,8},{73... | collective-permute-start | bytes 5898248 | tf_op jit(solution)/shard_map/ppermute | solution.py:534
  377.9 5.6 %collective-permute-start.45 = (bf16[80,1024]{1,0:T(8,128)(2,1)S(1)}, bf16[80,1024]{1,0:T(8,128)(2,1)S(1)}, u32[]{:S(2)}, u32[]{:S(2)}) collective-permute-start(bf16[80,1024]{1,0:T(8,128)(2,1)S(1)} %copy-done.59), channel_id=1, source_target_pairs={{0,64},{1,65},{2,66},{3,67},{4,68},{5,69},{6,70},{7,71},{8,72},{9,... | collective-permute-start | bytes 491528 | tf_op jit(solution)/shard_map/ppermute | solution.py:530
  382.2 8.2 %collective-permute-start.44 = (bf16[80,1024]{1,0:T(8,128)(2,1)S(1)}, bf16[80,1024]{1,0:T(8,128)(2,1)S(1)}, u32[]{:S(2)}, u32[]{:S(2)}) collective-permute-start(bf16[80,1024]{1,0:T(8,128)(2,1)S(1)} %get-tuple-element.127.r0), channel_id=1, source_target_pairs={{64,0},{65,1},{66,2},{67,3},{68,4},{69,5},{70,6},{71,7},{72,8},{73... | collective-permute-start | bytes 491528 | tf_op jit(solution)/shard_map/ppermute | solution.py:534
  383.5 48.9 %collective-permute-start.51 = (bf16[2,2,320,768]{3,2,1,0:T(8,128)(2,1)}, bf16[2,2,320,768]{3,2,1,0:T(8,128)(2,1)}, u32[]{:S(2)}, u32[]{:S(2)}) collective-permute-start(bf16[2,2,320,768]{3,2,1,0:T(8,128)(2,1)} %get-tuple-element.134.f1), channel_id=1, source_target_pairs={{0,64},{1,65},{2,66},{3,67},{4,68},{5,69},{6,70},{7,71},{8,72},{9,... | collective-permute-start | bytes 5898248 | tf_op jit(solution)/shard_map/ppermute | solution.py:530
  387.8 49.3 %collective-permute-start.53 = (bf16[2,2,320,768]{3,2,1,0:T(8,128)(2,1)}, bf16[2,2,320,768]{3,2,1,0:T(8,128)(2,1)}, u32[]{:S(2)}, u32[]{:S(2)}) collective-permute-start(bf16[2,2,320,768]{3,2,1,0:T(8,128)(2,1)} %get-tuple-element.136.b1), channel_id=1, source_target_pairs={{0,64},{1,65},{2,66},{3,67},{4,68},{5,69},{6,70},{7,71},{8,72},{9,... | collective-permute-start | bytes 5898248 | tf_op jit(solution)/shard_map/ppermute | solution.py:530
  390.4 46.8 %collective-permute-start.52 = (bf16[2,2,320,768]{3,2,1,0:T(8,128)(2,1)}, bf16[2,2,320,768]{3,2,1,0:T(8,128)(2,1)}, u32[]{:S(2)}, u32[]{:S(2)}) collective-permute-start(bf16[2,2,320,768]{3,2,1,0:T(8,128)(2,1)} %get-tuple-element.135.b0), channel_id=1, source_target_pairs={{64,0},{65,1},{66,2},{67,3},{68,4},{69,5},{70,6},{71,7},{72,8},{73... | collective-permute-start | bytes 5898248 | tf_op jit(solution)/shard_map/ppermute | solution.py:534
  396.1 34.1 %all-to-all-start.8 = ((bf16[16,64,768]{2,1,0:T(8,128)(2,1)}), bf16[16,64,768]{2,1,0:T(8,128)(2,1)S(1)}, u32[]{:S(2)}, u32[]{:S(2)}) async-start(bf16[16,64,768]{2,1,0:T(8,128)(2,1)} %shard_map.190), calls=%async_computation.8 | async-start | bytes 3145728 | tf_op jit(solution)/shard_map/all_to_all | solution.py:709
  415.6 6.1 %collective-permute-start.36 = (bf16[64,768]{1,0:T(8,128)(2,1)S(1)}, bf16[64,768]{1,0:T(8,128)(2,1)S(1)}, u32[]{:S(2)}, u32[]{:S(2)}) collective-permute-start(bf16[64,768]{1,0:T(8,128)(2,1)S(1)} %copy-done.79), channel_id=1, source_target_pairs={{0,2},{1,3},{2,0},{3,1},{4,6},{5,7},{6,4},{7,5},{8,10},{9,11},{10,... | collective-permute-start | bytes 294920 | tf_op jit(solution)/shard_map/ppermute | solution.py:510
  421.7 6.3 %collective-permute-start.37 = (bf16[64,768]{1,0:T(8,128)(2,1)S(1)}, bf16[64,768]{1,0:T(8,128)(2,1)S(1)}, u32[]{:S(2)}, u32[]{:S(2)}) collective-permute-start(bf16[64,768]{1,0:T(8,128)(2,1)S(1)} %copy-done.77), channel_id=1, source_target_pairs={{0,1},{1,2},{2,3},{3,0},{4,5},{5,6},{6,7},{7,4},{8,9},{9,10},{10,1... | collective-permute-start | bytes 294920 | tf_op jit(solution)/shard_map/ppermute | solution.py:510
  432.4 22.0 %collective-permute-start.46 = (f32[16,768]{1,0:T(8,128)S(1)}, f32[16,768]{1,0:T(8,128)S(1)}, u32[]{:S(2)}, u32[]{:S(2)}) collective-permute-start(f32[16,768]{1,0:T(8,128)S(1)} %get-tuple-element.165), channel_id=1, source_target_pairs={{0,1},{1,2},{2,3},{3,0},{4,5},{5,6},{6,7},{7,4},{8,9},{9,10},{10,1... | collective-permute-start | bytes 147464 | tf_op jit(solution)/shard_map/ppermute | solution.py:510
  432.4 21.9 %collective-permute-start.47 = (f32[16,768]{1,0:T(8,128)S(1)}, f32[16,768]{1,0:T(8,128)S(1)}, u32[]{:S(2)}, u32[]{:S(2)}) collective-permute-start(f32[16,768]{1,0:T(8,128)S(1)} %get-tuple-element.164), channel_id=1, source_target_pairs={{0,2},{1,3},{2,0},{3,1},{4,6},{5,7},{6,4},{7,5},{8,10},{9,11},{10,... | collective-permute-start | bytes 147464 | tf_op jit(solution)/shard_map/ppermute | solution.py:510
  435.9 18.5 %collective-permute-start.48 = (f32[16,768]{1,0:T(8,128)S(1)}, f32[16,768]{1,0:T(8,128)S(1)}, u32[]{:S(2)}, u32[]{:S(2)}) collective-permute-start(f32[16,768]{1,0:T(8,128)S(1)} %get-tuple-element.163), channel_id=1, source_target_pairs={{0,3},{1,0},{2,1},{3,2},{4,7},{5,4},{6,5},{7,6},{8,11},{9,8},{10,9... | collective-permute-start | bytes 147464 | tf_op jit(solution)/shard_map/ppermute | solution.py:510
  449.5 12.9 %collective-permute-start.49 = (f32[16,768]{1,0:T(8,128)S(1)}, f32[16,768]{1,0:T(8,128)S(1)}, u32[]{:S(2)}, u32[]{:S(2)}) collective-permute-start(f32[16,768]{1,0:T(8,128)S(1)} %get-tuple-element.131), channel_id=1, source_target_pairs={{0,0},{1,16},{2,32},{3,48},{4,1},{5,17},{6,33},{7,49},{8,2},{9,18}... | collective-permute-start | bytes 147464 | tf_op jit(solution)/shard_map/ppermute | solution.py:727
  (97 other events, 910.7 us)
